TPU v7x, 256 devices: a whole 4x4x8 slice. The times are simulated.
256 devices in a mesh: vir: 32 (over x, z), occ: 4 (over y), rep: 2 (over core).
Axes of the slice: x: 4, y: 4, z: 8, core: 2. Of those that a mesh axis runs over, the one named last changes fastest.
Arguments:
- amplitudes: float32 [256, 64, 4096], P('vir', ('occ', 'rep')), may hold values from -6 to 6
- integrals: float32 [384, 512, 4096], P('vir', None, ('occ', 'rep')), may hold values from -0.005859375 to 0.005859375
- block_owner: int32 [256], replicated, may hold values from 0 to 31, as said below
Outputs:
- ladder: float32 [64, 512], P('occ', 'rep')
Inputs may be any that keep to these rules, and one draw needn't show every extreme that they name: `block_owner`: blocks 8 * s to 8 * s + 7 start on vir index s. No vir index owns more than 12 blocks and some owns exactly 12; slots beyond an index's count are unused. No vir index's starting blocks name one owner more than 2 times, and each names some owner exactly 2 times.
All inputs are finite; a program needn't handle non-finite values.
Results may differ from a plain program's by a relative error of at most 0.0001.
Values sent between devices are 32-bit elements; how exact they have to be, the bound alone decides.
No kernel may reach another device: no remote copies, remote signals or barrier semaphores. Data moves between devices by JAX's collectives and lax.ppermute only.
A program may use at most 128 MiB of HBM per device.

v0:
```python
import jax
import jax.numpy as jnp
from jax import lax
from jax.sharding import PartitionSpec as P


def block_ranks(owners, blocks_dev):
    block_ids = jnp.arange(owners.shape[0], dtype=jnp.int32)
    earlier = block_ids[None, :] < block_ids[:, None]
    same_owner = owners[None, :] == owners[:, None]
    same_source = block_ids[None, :] // blocks_dev == block_ids[:, None] // blocks_dev
    owner_rank = jnp.sum(jnp.where(same_owner & earlier, 1, 0), axis=1).astype(jnp.int32)
    src_rank = jnp.sum(jnp.where(same_owner & earlier & same_source, 1, 0), axis=1).astype(
        jnp.int32
    )
    return (owner_rank, src_rank)


def contract(owned, integrals):
    return jnp.einsum(
        "vpx,vax->pa",
        owned,
        integrals,
        precision=lax.Precision.HIGHEST,
        preferred_element_type=jnp.float32,
    )


def on_device(amplitudes, integrals, block_owner):
    vir_count = lax.axis_size("vir")
    blocks_dev = amplitudes.shape[0]
    slot_count = integrals.shape[0]
    capacity = max(2, 3 * blocks_dev // (2 * vir_count))
    vir_index = lax.axis_index("vir")
    owner_rank, src_rank = block_ranks(block_owner, blocks_dev)
    block_ids = jnp.arange(block_owner.shape[0], dtype=jnp.int32)
    is_mine = block_owner == vir_index
    slot_pick = is_mine[None, :] & (
        owner_rank[None, :] == jnp.arange(slot_count, dtype=jnp.int32)[:, None]
    )
    slot_live = jnp.sum(jnp.where(slot_pick, 1, 0), axis=1)
    chosen = jnp.sum(jnp.where(slot_pick, block_ids[None, :], 0), axis=1)
    flat_index = chosen // blocks_dev * capacity + src_rank[chosen]
    slot_mask = slot_live.astype(jnp.float32)[:, None, None]
    local_ids = vir_index * blocks_dev + jnp.arange(blocks_dev, dtype=jnp.int32)
    target = block_owner[local_ids]
    target_rank = src_rank[local_ids]
    target_hit = (
        target[None, None, :] == jnp.arange(vir_count, dtype=jnp.int32)[:, None, None]
    ) & (target_rank[None, None, :] == jnp.arange(capacity, dtype=jnp.int32)[None, :, None])
    send_index = jnp.sum(
        jnp.where(target_hit, jnp.arange(blocks_dev, dtype=jnp.int32)[None, None, :], 0), axis=2
    )
    send_live = jnp.sum(jnp.where(target_hit, 1, 0), axis=2).astype(jnp.float32)
    outgoing = jnp.take(amplitudes, send_index, axis=0) * send_live[:, :, None, None]
    arrived = lax.all_to_all(outgoing, "vir", split_axis=0, concat_axis=0, tiled=True)
    row_stack = arrived.reshape((arrived.shape[0] * arrived.shape[1],) + arrived.shape[2:])
    owned = jnp.take(row_stack, flat_index, axis=0) * slot_mask
    owned = lax.all_to_all(owned, ("occ", "rep"), split_axis=2, concat_axis=1, tiled=True)
    partial_value = contract(owned, integrals)
    rep_part = lax.psum_scatter(partial_value, "rep", scatter_dimension=1, tiled=True)
    pair_part = lax.psum_scatter(rep_part, "occ", scatter_dimension=0, tiled=True)
    return lax.psum(pair_part, "vir")


def solution(mesh):
    in_specs = (P("vir", ("occ", "rep"), None), P("vir", None, ("occ", "rep")), P())
    out_specs = P("occ", "rep")
    return jax.shard_map(
        on_device, mesh=mesh, in_specs=in_specs, out_specs=out_specs, check_vma=False
    )
```

profile of v0, /device:TPU:0, one launch (start us, length us, event | category | flops | bytes accessed | tf_op | source)
XLA Modules:
  0.0 531.7 jit_solution(18139110158587541731)
XLA Ops:
  6.5 0.0 copy-start
  6.6 1.0 select_reduce_fusion.1
  7.6 1.3 gather_fusion.1
  8.9 0.6 gather_fusion.2
  9.6 0.1 iota_compare_fusion.2
  9.7 0.1 fusion.8
  9.8 0.1 copy.20
  9.9 0.1 reshape.278
  10.0 0.1 copy.19
  10.1 0.1 copy.21
  10.2 0.0 copy-done
  10.2 4.3 gather_fusion.3
  14.5 8.5 %select_multiply_fusion = f32[32,2,8,4096]{3,2,1,0:T(8,128)} fusion(f32[32,2,8,4096]{3,2,1,0:T(8,128)} %bitcast.42, f32[32,2]{1,0:T(8,128)S(1)} %copy.21, pred[32,2]{1,0:T(8,128)(4,1)S(1)} %copy.19), kind=kLoop, calls=%fused_computation.5 | loop fusion | flops 4194304 | bytes 16777536 | tf_op jit(solution)/shard_map/mul | solution.py:55
  22.9 0.0 copy-start.2
  22.9 9.8 %all-to-all-start = ((f32[32,2,8,4096]{3,2,1,0:T(8,128)}), f32[32,2,8,4096]{3,2,1,0:T(8,128)}, u32[]{:S(2)}, u32[]{:S(2)}) async-start(f32[32,2,8,4096]{3,2,1,0:T(8,128)} %select_multiply_fusion), calls=%async_computation | async-start | bytes 16777216 | tf_op jit(solution)/shard_map/all_to_all | solution.py:56
  32.8 0.0 reduce-scatter.3.cloned.1.call-start
  32.8 0.0 copy-done.2
  32.9 0.1 select_reduce_fusion.2
  33.0 0.7 gather_fusion
  33.7 187.9 %all-to-all-done = f32[32,2,8,4096]{3,2,1,0:T(8,128)} async-done(((f32[32,2,8,4096]{3,2,1,0:T(8,128)}), f32[32,2,8,4096]{3,2,1,0:T(8,128)}, u32[]{:S(2)}, u32[]{:S(2)}) %all-to-all-start) | async-done | bytes 8388640 | tf_op jit(solution)/shard_map/all_to_all | solution.py:56
  221.6 5.3 gather_fusion.4
  226.9 1.6 select_multiply_fusion.1
  228.5 9.0 %copy.22 = f32[12,8,4096]{0,1,2:T(8,128)} copy(f32[12,8,4096]{2,1,0:T(8,128)S(1)} %select_multiply_fusion.1) | data formatting | bytes 3145728 | tf_op jit(solution)/shard_map/mul | solution.py:58
  237.5 18.2 %reshape.294 = f32[8,1,49152]{2,1,0:T(1,128)S(1)} reshape(f32[4096,8,12]{2,1,0:T(8,128)} %bitcast.40) | data formatting | bytes 3145728
  255.7 26.2 %all_to_all.23 = f32[8,1,49152]{2,1,0:T(1,128)} all-to-all(f32[8,1,49152]{2,1,0:T(1,128)S(1)} %reshape.294), channel_id=1, replica_groups=mesh['vir'=32,'occ'=4,'rep'=2] {'occ','rep'}, dimensions={0} | all-to-all | bytes 3145728 | tf_op jit(solution)/shard_map/all_to_all | solution.py:59
  281.9 0.5 broadcast.330
  282.4 5.8 %reduce = f32[8,49152]{1,0:T(8,128)S(1)} reduce(f32[8,1,49152]{2,1,0:T(1,128)} %all_to_all.23, f32[]{:T(128)} %broadcast.330), dimensions={1}, to_apply=%all_to_all.17.reduce_sub_computation | reduce | bytes 3145732 | tf_op jit(solution)/shard_map/all_to_all | solution.py:59
  288.2 24.4 %reshape.295 = f32[4096,8,12]{2,1,0:T(8,128)} reshape(f32[8,49152]{1,0:T(8,128)S(1)} %reduce) | data formatting | bytes 3145728
  312.6 0.0 copy-start.1
  312.6 10.2 %copy.23 = f32[12,8,8,512]{3,1,2,0:T(8,128)S(1)} copy(f32[12,8,8,512]{0,1,3,2:T(8,128)} %bitcast.41) | data formatting | bytes 3145728 | tf_op jit(solution)/shard_map/all_to_all | solution.py:59
  322.8 15.7 %fusion.2 = f32[64,512]{1,0:T(8,128)} fusion(f32[12,512,512]{2,1,0:T(8,128)} %param.4, f32[12,8,8,512]{3,1,2,0:T(8,128)S(1)} %copy.23), kind=kOutput, calls=%fused_computation.9 | convolution fusion | flops 2415919104 | bytes 14286848 | tf_op jit(solution)/shard_map/vpx,vax->pa/dot_general | solution.py:20
  338.5 0.0 reduce-scatter.3.cloned.1.call-update
  338.5 0.0 reduce-scatter.5.cloned.1.call-start
  338.6 16.5 %reduce-scatter.3.cloned.1.call-done = f32[64,256]{1,0:T(8,128)} async-done(((f32[64,512]{1,0:T(8,128)}), f32[64,256]{1,0:T(8,128)}) %reduce-scatter.3.cloned.1.call-update) | async-done | bytes 65552 | tf_op jit(solution)/shard_map/reduce_scatter | solution.py:61
  355.1 0.0 reduce-scatter.5.cloned.1.call-update
  355.1 26.6 %reduce-scatter.5.cloned.1.call-done = f32[16,256]{1,0:T(8,128)} async-done(((f32[64,256]{1,0:T(8,128)}), f32[16,256]{1,0:T(8,128)}) %reduce-scatter.5.cloned.1.call-update) | async-done | bytes 16400 | tf_op jit(solution)/shard_map/reduce_scatter | solution.py:62
  381.8 143.1 %psum.7 = f32[16,256]{1,0:T(8,128)} all-reduce(f32[16,256]{1,0:T(8,128)} %reduce-scatter.5.cloned.1.call-done), channel_id=1, replica_groups=mesh['vir'=32,'occ'=4,'rep'=2] {'vir'}, use_global_device_ids=true, to_apply=%region_8.9 | all-reduce | flops 4096 | bytes 32768 | tf_op jit(solution)/shard_map/psum | solution.py:63
  524.9 0.0 copy-done.1
  (15 shorter events, 0.1 us)
Async XLA Ops:
  6.5 3.6 copy-start
  22.9 9.9 %copy-start.2 = (s32[256]{0:T(256)S(1)}, s32[256]{0:T(256)}, u32[]{:S(2)}) copy-start(s32[256]{0:T(256)} %param.5) | copy-start | bytes 3076
  22.9 198.6 %all-to-all-start = ((f32[32,2,8,4096]{3,2,1,0:T(8,128)}), f32[32,2,8,4096]{3,2,1,0:T(8,128)}, u32[]{:S(2)}, u32[]{:S(2)}) async-start(f32[32,2,8,4096]{3,2,1,0:T(8,128)} %select_multiply_fusion), calls=%async_computation | async-start | bytes 16777216 | tf_op jit(solution)/shard_map/all_to_all | solution.py:56
  32.8 322.3 %reduce-scatter.3.cloned.1.call-start = ((), (), s32[]{:S(2)}) async-start(), calls=%async_computation.4 | async-start | bytes 196608 | tf_op jit(solution)/shard_map/reduce_scatter | solution.py:61
  312.6 212.3 %copy-start.1 = (f32[8,8,4096]{2,1,0:T(8,128)S(1)}, f32[8,8,4096]{2,1,0:T(8,128)}, u32[]{:S(2)}) copy-start(f32[8,8,4096]{2,1,0:T(8,128)} %param.3) | copy-start | bytes 3145732
  338.5 43.3 %reduce-scatter.5.cloned.1.call-start = ((), (), s32[]{:S(2)}) async-start(), calls=%async_computation.5 | async-start | bytes 81920 | tf_op jit(solution)/shard_map/reduce_scatter | solution.py:62
Sparse Core Ops, SparseCore 0:
  338.7 16.4 reduce-scatter.2
  357.6 24.1 reduce-scatter.4
where the time goes:
time: 532 us
  waiting for transfers between devices  231 us (43%)
  blocking collectives  169 us (32%)
  local copies, waits for them, and re-layouts  74.9 us (14%)
  other arithmetic  17.3 us (3%)
  matrix products  15.7 us (3%)
  between operations  13.5 us (3%)
  starting transfers between devices  9.92 us (2%)
    all_to_all x1, waiting for transfers between devices, on_device(): lax.all_to_all(outgoing, 'vir', split_axis=0, concat_axis=0, tiled=True)  188 us
    psum x1, blocking collectives, on_device(): return lax.psum(pair_part, 'vir')  143 us
    unnamed x8, local copies, waits for them, and re-layouts  42.6 us
    reduce_scatter x1, waiting for transfers between devices, on_device(): lax.psum_scatter(rep_part, 'occ', scatter_dimension=0, tiled=True)  26.6 us
    all_to_all x1, blocking collectives, on_device(): lax.all_to_all(owned, ('occ', 'rep'), split_axis=2, concat_axis=1, tiled=...  26.2 us
    reduce_scatter x1, waiting for transfers between devices, on_device(): lax.psum_scatter(partial_value, 'rep', scatter_dimension=1, tiled=True)  16.5 us
    dot_general x1, matrix products, contract(): jnp.einsum('vpx,vax->pa', owned, integrals, precision=lax.Precision.HIGHE...  15.7 us
    all_to_all x2, local copies, waits for them, and re-layouts, on_device(): lax.all_to_all(owned, ('occ', 'rep'), split_axis=2, concat_axis=1, tiled=...  10.7 us
  transfers between devices with their start and end apart: 3, of which 3 were waited for; matrix products, arithmetic and copies ran while one was open for 0% of the time, Pallas kernels for 0%

commit v1 on v0

v1 whole, which is shorter than its diff:
```python
import functools

import jax
import jax.numpy as jnp
from jax import lax
from jax.experimental import pallas as pl
from jax.experimental.pallas import tpu as pltpu
from jax.sharding import PartitionSpec as P

ALL = ("vir", "occ", "rep")
VIR = 32
GRP = 8
BLKS = 8
SLOTS = 12
LANE = 128
MIB = 1 << 20


def slot_of_block(owners):
    ids = jnp.arange(owners.shape[0], dtype=jnp.int32)
    earlier = ids[None, :] < ids[:, None]
    same = owners[None, :] == owners[:, None]
    rank = jnp.sum(jnp.where(same & earlier, 1, 0), axis=1).astype(jnp.int32)
    return owners * SLOTS + rank


def spread_kernel(amp_ref, out_ref):
    for blk in range(BLKS):
        for chunk in range(32):
            part, quarter = chunk // 4, chunk % 4
            out_ref[pl.ds((quarter * GRP + part) * BLKS + blk, 8, stride=4 * GRP * BLKS), :] = (
                amp_ref[pl.ds(blk * 8, 8), pl.ds(chunk * LANE, LANE)]
            )


def spread(amp):
    return pl.pallas_call(
        spread_kernel,
        out_shape=jax.ShapeDtypeStruct((VIR * GRP * BLKS, LANE), jnp.float32),
        in_specs=[pl.BlockSpec(memory_space=pltpu.VMEM)],
        out_specs=pl.BlockSpec(memory_space=pltpu.VMEM),
        compiler_params=pltpu.CompilerParams(vmem_limit_bytes=8 * MIB),
        cost_estimate=pl.CostEstimate(flops=0, bytes_accessed=2 * MIB, transcendentals=0),
        name="spread",
    )(amp)


def route_kernel(slot_ref, got_ref, out_ref):
    def clear(i, carry):
        out_ref[pl.ds(i * SLOTS, SLOTS)] = jnp.zeros((SLOTS, GRP, LANE), jnp.float32)
        return carry

    lax.fori_loop(0, VIR, clear, 0)

    for source in range(VIR):
        for blk in range(BLKS):
            out_ref[slot_ref[source * BLKS + blk]] = got_ref[
                pl.ds(source * GRP * BLKS + blk, GRP, stride=BLKS), :
            ]


def route(slot, got):
    return pl.pallas_call(
        route_kernel,
        out_shape=jax.ShapeDtypeStruct((VIR * SLOTS, GRP, LANE), jnp.float32),
        in_specs=[
            pl.BlockSpec(memory_space=pltpu.SMEM),
            pl.BlockSpec(memory_space=pltpu.VMEM),
        ],
        out_specs=pl.BlockSpec(memory_space=pltpu.VMEM),
        compiler_params=pltpu.CompilerParams(vmem_limit_bytes=8 * MIB),
        cost_estimate=pl.CostEstimate(flops=0, bytes_accessed=3 * MIB, transcendentals=0),
        name="route",
    )(slot, got)


def split(value):
    high = value.astype(jnp.bfloat16)
    return high, (value - high.astype(jnp.float32)).astype(jnp.bfloat16)


def dot_nt(left, right):
    return lax.dot_general(
        left, right, (((1,), (1,)), ((), ())), preferred_element_type=jnp.float32
    )


def contract_kernel(place_ref, amp_ref, int_ref, *refs):
    outs, (acc, tiles, ordered) = refs[:8], refs[8:]
    slot = pl.program_id(0)

    @pl.when(slot == 0)
    def _():
        acc[...] = jnp.zeros_like(acc)

    rows = jnp.concatenate(
        [amp_ref[:, q, slot].reshape(64, LANE) for q in range(4)], axis=1
    )
    a_high, a_low = split(rows)
    b_high, b_low = split(int_ref[0])
    both = dot_nt(jnp.concatenate([a_high, a_low], axis=0), b_high)
    acc[...] += both[:64] + both[64:] + dot_nt(a_high, b_low)

    @pl.when(slot == SLOTS - 1)
    def _():
        occ, rep = place_ref[0], place_ref[1]
        for tile in range(4):
            tiles[tile] = acc[:, pl.ds(tile * LANE, LANE)]
        for tile in range(4):
            for group in range(GRP):
                ordered[tile // 2, pl.ds(group * 8, 8), pl.ds(tile % 2 * LANE, LANE)] = tiles[
                    tile, pl.ds(group, 8, stride=GRP), :
                ]
        for k in range(8):
            row = lax.rem(occ + k // 2, 4) * 16
            half = rep if k % 2 == 0 else 1 - rep
            outs[k][...] = ordered[half, pl.ds(pl.multiple_of(row, 16), 16), :]


def contract(place, amp, integrals):
    piece = jax.ShapeDtypeStruct((16, 256), jnp.float32)
    return pl.pallas_call(
        contract_kernel,
        grid=(SLOTS,),
        out_shape=[piece] * 8,
        in_specs=[
            pl.BlockSpec(memory_space=pltpu.SMEM),
            pl.BlockSpec((8, 4, SLOTS, GRP, LANE), lambda i: (0, 0, 0, 0, 0)),
            pl.BlockSpec((1, 512, 512), lambda i: (i, 0, 0)),
        ],
        out_specs=[pl.BlockSpec((16, 256), lambda i: (0, 0))] * 8,
        scratch_shapes=[
            pltpu.VMEM((64, 512), jnp.float32),
            pltpu.VMEM((4, 64, LANE), jnp.float32),
            pltpu.VMEM((2, 64, 256), jnp.float32),
        ],
        compiler_params=pltpu.CompilerParams(vmem_limit_bytes=16 * MIB),
        cost_estimate=pl.CostEstimate(
            flops=6 * 64 * 512 * 6144, bytes_accessed=14 * MIB, transcendentals=0
        ),
        name="contract",
    )(place, amp, integrals)


def sum_ring_kernel(size, place_ref, *refs):
    ins, out_ref, held = refs[:size], refs[size], refs[size + 1]
    for k in range(size):
        held[lax.rem(place_ref[0] + size - k, size)] = ins[k][...]
    total = held[0]
    for k in range(1, size):
        total = total + held[k]
    out_ref[...] = total


def sum_ring(place, pieces):
    size = len(pieces)
    return pl.pallas_call(
        functools.partial(sum_ring_kernel, size),
        out_shape=jax.ShapeDtypeStruct((16, 256), jnp.float32),
        in_specs=[pl.BlockSpec(memory_space=pltpu.SMEM)]
        + [pl.BlockSpec(memory_space=pltpu.VMEM)] * size,
        out_specs=pl.BlockSpec(memory_space=pltpu.VMEM),
        scratch_shapes=[pltpu.VMEM((size, 16, 256), jnp.float32)],
        compiler_params=pltpu.CompilerParams(vmem_limit_bytes=4 * MIB),
        name="sum_ring",
    )(place, *pieces)


def group_shift(k):
    return [
        (o * 2 + r, (o + k // 2) % 4 * 2 + (r ^ (k % 2))) for o in range(4) for r in range(2)
    ]


def x_shift(k):
    return [(x * 8 + z, (x + k) % 4 * 8 + z) for x in range(4) for z in range(8)]


def z_shift(k):
    return [(x * 8 + z, x * 8 + (z + k) % 8) for x in range(4) for z in range(8)]


def on_device(amplitudes, integrals, block_owner):
    vir, occ, rep = (lax.axis_index(name) for name in ALL)
    slot = slot_of_block(block_owner)
    sent = spread(amplitudes.reshape(BLKS * 8, 4096))
    sent = sent.reshape(VIR * GRP, BLKS, LANE)
    got = lax.all_to_all(sent, ALL, split_axis=0, concat_axis=0, tiled=True)
    routed = route(slot, got.reshape(VIR * GRP * BLKS, LANE))
    owned = lax.all_to_all(
        routed.reshape(VIR, SLOTS * GRP, LANE), "vir", split_axis=0, concat_axis=0, tiled=True
    )
    pieces = contract(
        jnp.stack([occ, rep]), owned.reshape(8, 4, SLOTS, GRP, LANE), integrals
    )
    arrived = [pieces[0]] + [
        lax.ppermute(pieces[k], ("occ", "rep"), group_shift(k)) for k in range(1, 8)
    ]
    total = sum(arrived[1:], arrived[0])
    total = sum_ring(
        (vir // 8)[None],
        [total] + [lax.ppermute(total, "vir", x_shift(k)) for k in range(1, 4)],
    )
    return sum_ring(
        (vir % 8)[None],
        [total] + [lax.ppermute(total, "vir", z_shift(k)) for k in range(1, 8)],
    )


def solution(mesh):
    in_specs = (P("vir", ("occ", "rep"), None), P("vir", None, ("occ", "rep")), P())
    out_specs = P("occ", "rep")
    return jax.shard_map(
        on_device, mesh=mesh, in_specs=in_specs, out_specs=out_specs, check_vma=False
    )
```

time: 532 us -> 143 us (0.27)
  blocking collectives: 169 us -> 0 us
  waiting for transfers between devices: 231 us -> 79.7 us
  local copies, waits for them, and re-layouts: 74.9 us -> 5.8 us
  starting transfers between devices: 9.92 us -> 44.9 us
  other arithmetic: 17.3 us -> 0.27 us
  matrix products: 15.7 us -> 0 us
  between operations: 13.5 us -> 0.08 us
  Pallas kernels: 0 us -> 11.2 us
    psum x1 -> x0, blocking collectives: 143 us -> none  [on_device(): return lax.psum(pair_part, 'vir')]
    all_to_all x1 -> x2, waiting for transfers between devices: 188 us -> 68.3 us  [the longest x1 39 us: on_device(): lax.all_to_all(routed.reshape(VIR, SLOTS * GRP, LANE), 'vir', split_axis=...]
    reduce_scatter x2 -> x0, waiting for transfers between devices: 43.2 us -> none  [the longest x1 26.6 us: on_device(): lax.psum_scatter(rep_part, 'occ', scatter_dimension=0, tiled=True)]
    unnamed x8 -> x6, local copies, waits for them, and re-layouts: 42.6 us -> 5.8 us
    all_to_all x1 -> x0, blocking collectives: 26.2 us -> none  [on_device(): lax.all_to_all(owned, ('occ', 'rep'), split_axis=2, concat_axis=1, tiled=...]
    ppermute x0 -> x17, starting transfers between devices: none -> 25.4 us  [the longest x7 14.9 us: on_device(): lax.ppermute(total, 'vir', z_shift(k))]
    dot_general x1 -> x0, matrix products: 15.7 us -> none  [contract(): jnp.einsum('vpx,vax->pa', owned, integrals, precision=lax.Precision.HIGHE...]
    gather x5 -> x0, local copies, waits for them, and re-layouts: 12.2 us -> none  [the longest x1 5.26 us: on_device(): owned = jnp.take(row_stack, flat_index, axis=0) * slot_mask]
  transfers between devices with their start and end apart: 3 -> 19, of which waited for: 3 -> 11; matrix products, arithmetic and copies ran while one was open for 0% -> 0% of each run, Pallas kernels for 0% -> 0%
where the time goes in v1:
time: 143 us; the launch traced here: 142 us
  waiting for transfers between devices  79.7 us (56%)
  starting transfers between devices  44.9 us (31%)
  Pallas kernels  11.2 us (8%)
  local copies, waits for them, and re-layouts  5.8 us (4%)
    all_to_all x1, waiting for transfers between devices, on_device(): lax.all_to_all(routed.reshape(VIR, SLOTS * GRP, LANE), 'vir', split_axis=...  39 us
    all_to_all x1, waiting for transfers between devices, on_device(): got = lax.all_to_all(sent, ALL, split_axis=0, concat_axis=0, tiled=True)  29.4 us
    ppermute x7, starting transfers between devices, on_device(): lax.ppermute(total, 'vir', z_shift(k))  14.9 us
    all_to_all x1, starting transfers between devices, on_device(): got = lax.all_to_all(sent, ALL, split_axis=0, concat_axis=0, tiled=True)  14.6 us
    ppermute x7, starting transfers between devices, on_device(): lax.ppermute(pieces[k], ('occ', 'rep'), group_shift(k))  8.18 us
    pallas_call x1, Pallas kernels, contract(): pl.pallas_call(contract_kernel, grid=(SLOTS,), out_shape=[piece] * 8, in_...  6.48 us
    unnamed x6, local copies, waits for them, and re-layouts  5.8 us
    ppermute x7, waiting for transfers between devices, on_device(): lax.ppermute(total, 'vir', z_shift(k))  4.95 us
  transfers between devices with their start and end apart: 19, of which 11 were waited for; matrix products, arithmetic and copies ran while one was open for 0% of the time, Pallas kernels for 0%

profile of v1, /device:TPU:0, one launch (start us, length us, event | category | flops | bytes accessed | tf_op | source)
XLA Modules:
  0.0 142.0 jit_solution(11212664221668567864)
XLA Ops:
  0.0 0.0 copy-start.1
  0.0 1.2 copy-done.1
  1.2 2.0 %spread.1 = f32[2048,128]{1,0:T(8,128)} custom-call(f32[64,4096]{1,0:T(8,128)S(1)} %bitcast.11), custom_call_target="tpu_custom_call" | custom-call | bytes 2097152 | tf_op jit(solution)/shard_map/spread/pallas_call | solution.py:37
  3.2 0.0 copy-start.2
  3.2 14.6 %all-to-all-start = ((f32[256,8,128]{2,1,0:T(8,128)}), f32[256,8,128]{2,1,0:T(8,128)S(1)}, u32[]{:S(2)}, u32[]{:S(2)}) async-start(f32[256,8,128]{2,1,0:T(8,128)} %bitcast.5), calls=%async_computation | async-start | bytes 2097152 | tf_op jit(solution)/shard_map/all_to_all | solution.py:188
  17.8 0.0 copy-done.2
  17.8 0.2 select_reduce_fusion
  18.0 29.4 %all-to-all-done = f32[256,8,128]{2,1,0:T(8,128)S(1)} async-done(((f32[256,8,128]{2,1,0:T(8,128)}), f32[256,8,128]{2,1,0:T(8,128)S(1)}, u32[]{:S(2)}, u32[]{:S(2)}) %all-to-all-start) | async-done | bytes 1048608 | tf_op jit(solution)/shard_map/all_to_all | solution.py:188
  47.3 2.1 %route.1 = f32[384,8,128]{2,1,0:T(8,128)} custom-call(s32[256]{0:T(256)S(1)} %multiply_add_fusion.slot_ref, f32[2048,128]{1,0:T(8,128)S(1)} %bitcast.10), custom_call_target="tpu_custom_call" | custom-call | bytes 3145728 | tf_op jit(solution)/shard_map/route/pallas_call | solution.py:63
  49.5 4.9 %all-to-all-start.1 = ((f32[32,96,128]{2,1,0:T(8,128)}), f32[32,96,128]{2,1,0:T(8,128)S(1)}, u32[]{:S(2)}, u32[]{:S(2)}) async-start(f32[32,96,128]{2,1,0:T(8,128)} %bitcast.7), calls=%async_computation.1 | async-start | bytes 3145728 | tf_op jit(solution)/shard_map/all_to_all | solution.py:190
  54.4 0.1 pad_add_fusion.place_ref
  54.5 39.0 %all-to-all-done.1 = f32[32,96,128]{2,1,0:T(8,128)S(1)} async-done(((f32[32,96,128]{2,1,0:T(8,128)}), f32[32,96,128]{2,1,0:T(8,128)S(1)}, u32[]{:S(2)}, u32[]{:S(2)}) %all-to-all-start.1) | async-done | bytes 1572896 | tf_op jit(solution)/shard_map/all_to_all | solution.py:190
  93.4 0.0 copy-start
  93.4 4.6 %copy-done = f32[12,512,512]{2,1,0:T(8,128)S(1)} copy-done((f32[12,512,512]{2,1,0:T(8,128)S(1)}, f32[12,512,512]{2,1,0:T(8,128)}, u32[]{:S(2)}) %copy-start) | copy-done | bytes 12582936
  98.0 6.5 %contract.1 = (f32[16,256]{1,0:T(8,128)S(1)}, f32[16,256]{1,0:T(8,128)S(1)}, f32[16,256]{1,0:T(8,128)S(1)}, f32[16,256]{1,0:T(8,128)S(1)}, f32[16,256]{1,0:T(8,1...) custom-call(s32[2]{0:T(128)S(1)} %pad_add_fusion.place_ref, ...), custom_call_target="tpu_custom_call" | custom-call | flops 1207959552 | bytes 14680064 | tf_op jit(solution)/shard_map/contract/pallas_call | solution.py:122
  104.5 0.1 collective-permute-start
  104.6 1.0 collective-permute-start.1
  105.6 0.9 collective-permute-start.2
  106.5 2.7 %collective-permute-start.3 = (f32[16,256]{1,0:T(8,128)S(1)}, f32[16,256]{1,0:T(8,128)S(1)}, u32[]{:S(2)}, u32[]{:S(2)}) collective-permute-start(f32[16,256]{1,0:T(8,128)S(1)} %get-tuple-element.17), channel_id=1, source_target_pairs={{0,4},{1,5},{2,6},{3,7},{4,0},{5,1},{6,2},{7,3},{8,12},{9,13},{10,... | collective-permute-start | bytes 49160 | tf_op jit(solution)/shard_map/ppermute | solution.py:197
  109.2 0.5 collective-permute-start.4
  109.7 0.0 collective-permute-done
  109.7 2.1 %collective-permute-start.5 = (f32[16,256]{1,0:T(8,128)S(1)}, f32[16,256]{1,0:T(8,128)S(1)}, u32[]{:S(2)}, u32[]{:S(2)}) collective-permute-start(f32[16,256]{1,0:T(8,128)S(1)} %get-tuple-element.19), channel_id=1, source_target_pairs={{0,6},{1,7},{2,0},{3,1},{4,2},{5,3},{6,4},{7,5},{8,14},{9,15},{10,... | collective-permute-start | bytes 49160 | tf_op jit(solution)/shard_map/ppermute | solution.py:197
  111.8 0.0 collective-permute-done.1
  111.8 0.9 collective-permute-start.6
  112.7 0.0 collective-permute-done.2
  112.7 0.0 collective-permute-done.3
  112.7 1.1 collective-permute-done.4
  113.8 0.0 collective-permute-done.5
  113.8 1.1 collective-permute-done.6
  115.0 0.9 collective-permute-start.9
  115.8 0.5 collective-permute-start.8
  116.3 0.9 collective-permute-start.7
  117.2 1.5 %collective-permute-done.9.refs_3_ = f32[16,256]{1,0:T(8,128)S(1)} collective-permute-done((f32[16,256]{1,0:T(8,128)S(1)}, f32[16,256]{1,0:T(8,128)S(1)}, u32[]{:S(2)}, u32[]{:S(2)}) %collective-permute-start.9) | collective-permute-done | bytes 16416 | tf_op jit(solution)/shard_map/ppermute | solution.py:202
  118.8 2.3 %collective-permute-done.8.refs_2_ = f32[16,256]{1,0:T(8,128)S(1)} collective-permute-done((f32[16,256]{1,0:T(8,128)S(1)}, f32[16,256]{1,0:T(8,128)S(1)}, u32[]{:S(2)}, u32[]{:S(2)}) %collective-permute-start.8) | collective-permute-done | bytes 16416 | tf_op jit(solution)/shard_map/ppermute | solution.py:202
  121.1 0.4 collective-permute-done.7.refs_1_
  121.5 2.5 %collective-permute-start.16 = (f32[16,256]{1,0:T(8,128)S(1)}, f32[16,256]{1,0:T(8,128)S(1)}, u32[]{:S(2)}, u32[]{:S(2)}) collective-permute-start(f32[16,256]{1,0:T(8,128)S(1)} %sum_ring.2.refs_0_), channel_id=1, source_target_pairs={{0,56},{8,0},{16,8},{24,16},{32,24},{40,32},{48,40},{56,48},{64,12... | collective-permute-start | bytes 49160 | tf_op jit(solution)/shard_map/ppermute | solution.py:206
  123.9 1.4 collective-permute-start.15
  125.3 4.2 %collective-permute-start.14 = (f32[16,256]{1,0:T(8,128)S(1)}, f32[16,256]{1,0:T(8,128)S(1)}, u32[]{:S(2)}, u32[]{:S(2)}) collective-permute-start(f32[16,256]{1,0:T(8,128)S(1)} %sum_ring.2.refs_0_), channel_id=1, source_target_pairs={{0,40},{8,48},{16,56},{24,0},{32,8},{40,16},{48,24},{56,32},{64,10... | collective-permute-start | bytes 49160 | tf_op jit(solution)/shard_map/ppermute | solution.py:206
  129.5 2.2 %collective-permute-start.13 = (f32[16,256]{1,0:T(8,128)S(1)}, f32[16,256]{1,0:T(8,128)S(1)}, u32[]{:S(2)}, u32[]{:S(2)}) collective-permute-start(f32[16,256]{1,0:T(8,128)S(1)} %sum_ring.2.refs_0_), channel_id=1, source_target_pairs={{0,32},{8,40},{16,48},{24,56},{32,0},{40,8},{48,16},{56,24},{64,96... | collective-permute-start | bytes 49160 | tf_op jit(solution)/shard_map/ppermute | solution.py:206
  131.7 1.7 %collective-permute-start.12 = (f32[16,256]{1,0:T(8,128)S(1)}, f32[16,256]{1,0:T(8,128)S(1)}, u32[]{:S(2)}, u32[]{:S(2)}) collective-permute-start(f32[16,256]{1,0:T(8,128)S(1)} %sum_ring.2.refs_0_), channel_id=1, source_target_pairs={{0,24},{8,32},{16,40},{24,48},{32,56},{40,0},{48,8},{56,16},{64,88... | collective-permute-start | bytes 49160 | tf_op jit(solution)/shard_map/ppermute | solution.py:206
  133.4 0.0 collective-permute-done.16.refs_7_
  133.4 3.0 %collective-permute-start.11 = (f32[16,256]{1,0:T(8,128)S(1)}, f32[16,256]{1,0:T(8,128)S(1)}, u32[]{:S(2)}, u32[]{:S(2)}) collective-permute-start(f32[16,256]{1,0:T(8,128)S(1)} %sum_ring.2.refs_0_), channel_id=1, source_target_pairs={{0,16},{8,24},{16,32},{24,40},{32,48},{40,56},{48,0},{56,8},{64,80... | collective-permute-start | bytes 49160 | tf_op jit(solution)/shard_map/ppermute | solution.py:206
  136.4 0.0 collective-permute-done.15.refs_6_
  136.4 0.0 collective-permute-start.10
  136.4 0.0 collective-permute-done.14.refs_5_
  136.4 0.8 collective-permute-done.13.refs_4_
  137.2 1.3 collective-permute-done.12.refs_3_
  138.5 0.8 collective-permute-done.11.refs_2_
  139.3 2.1 %collective-permute-done.10.refs_1_ = f32[16,256]{1,0:T(8,128)S(1)} collective-permute-done((f32[16,256]{1,0:T(8,128)S(1)}, f32[16,256]{1,0:T(8,128)S(1)}, u32[]{:S(2)}, u32[]{:S(2)}) %collective-permute-start.10) | collective-permute-done | bytes 16416 | tf_op jit(solution)/shard_map/ppermute | solution.py:206
  141.4 0.6 sum_ring.3
  (3 shorter events, 0.0 us)
Async XLA Ops:
  0.0 1.2 copy-start.1
  3.2 14.6 %copy-start.2 = (s32[256]{0:T(256)S(1)}, s32[256]{0:T(256)}, u32[]{:S(2)}) copy-start(s32[256]{0:T(256)} %param.5) | copy-start | bytes 3076
  3.2 44.2 %all-to-all-start = ((f32[256,8,128]{2,1,0:T(8,128)}), f32[256,8,128]{2,1,0:T(8,128)S(1)}, u32[]{:S(2)}, u32[]{:S(2)}) async-start(f32[256,8,128]{2,1,0:T(8,128)} %bitcast.5), calls=%async_computation | async-start | bytes 2097152 | tf_op jit(solution)/shard_map/all_to_all | solution.py:188
  49.5 44.0 %all-to-all-start.1 = ((f32[32,96,128]{2,1,0:T(8,128)}), f32[32,96,128]{2,1,0:T(8,128)S(1)}, u32[]{:S(2)}, u32[]{:S(2)}) async-start(f32[32,96,128]{2,1,0:T(8,128)} %bitcast.7), calls=%async_computation.1 | async-start | bytes 3145728 | tf_op jit(solution)/shard_map/all_to_all | solution.py:190
  93.4 4.6 %copy-start = (f32[12,512,512]{2,1,0:T(8,128)S(1)}, f32[12,512,512]{2,1,0:T(8,128)}, u32[]{:S(2)}) copy-start(f32[12,512,512]{2,1,0:T(8,128)} %int_ref.1) | copy-start | bytes 37748740
  104.5 5.2 %collective-permute-start = (f32[16,256]{1,0:T(8,128)S(1)}, f32[16,256]{1,0:T(8,128)S(1)}, u32[]{:S(2)}, u32[]{:S(2)}) collective-permute-start(f32[16,256]{1,0:T(8,128)S(1)} %get-tuple-element.14), channel_id=1, source_target_pairs={{0,1},{1,0},{2,3},{3,2},{4,5},{5,4},{6,7},{7,6},{8,9},{9,8},{10,11... | collective-permute-start | bytes 49160 | tf_op jit(solution)/shard_map/ppermute | solution.py:197
  104.6 7.2 %collective-permute-start.1 = (f32[16,256]{1,0:T(8,128)S(1)}, f32[16,256]{1,0:T(8,128)S(1)}, u32[]{:S(2)}, u32[]{:S(2)}) collective-permute-start(f32[16,256]{1,0:T(8,128)S(1)} %get-tuple-element.15), channel_id=1, source_target_pairs={{0,2},{1,3},{2,4},{3,5},{4,6},{5,7},{6,0},{7,1},{8,10},{9,11},{10,... | collective-permute-start | bytes 49160 | tf_op jit(solution)/shard_map/ppermute | solution.py:197
  105.6 7.1 %collective-permute-start.2 = (f32[16,256]{1,0:T(8,128)S(1)}, f32[16,256]{1,0:T(8,128)S(1)}, u32[]{:S(2)}, u32[]{:S(2)}) collective-permute-start(f32[16,256]{1,0:T(8,128)S(1)} %get-tuple-element.16), channel_id=1, source_target_pairs={{0,3},{1,2},{2,5},{3,4},{4,7},{5,6},{6,1},{7,0},{8,11},{9,10},{10,... | collective-permute-start | bytes 49160 | tf_op jit(solution)/shard_map/ppermute | solution.py:197
  106.5 6.2 %collective-permute-start.3 = (f32[16,256]{1,0:T(8,128)S(1)}, f32[16,256]{1,0:T(8,128)S(1)}, u32[]{:S(2)}, u32[]{:S(2)}) collective-permute-start(f32[16,256]{1,0:T(8,128)S(1)} %get-tuple-element.17), channel_id=1, source_target_pairs={{0,4},{1,5},{2,6},{3,7},{4,0},{5,1},{6,2},{7,3},{8,12},{9,13},{10,... | collective-permute-start | bytes 49160 | tf_op jit(solution)/shard_map/ppermute | solution.py:197
  109.2 4.7 %collective-permute-start.4 = (f32[16,256]{1,0:T(8,128)S(1)}, f32[16,256]{1,0:T(8,128)S(1)}, u32[]{:S(2)}, u32[]{:S(2)}) collective-permute-start(f32[16,256]{1,0:T(8,128)S(1)} %get-tuple-element.18), channel_id=1, source_target_pairs={{0,5},{1,4},{2,7},{3,6},{4,1},{5,0},{6,3},{7,2},{8,13},{9,12},{10,... | collective-permute-start | bytes 49160 | tf_op jit(solution)/shard_map/ppermute | solution.py:197
  109.7 4.1 %collective-permute-start.5 = (f32[16,256]{1,0:T(8,128)S(1)}, f32[16,256]{1,0:T(8,128)S(1)}, u32[]{:S(2)}, u32[]{:S(2)}) collective-permute-start(f32[16,256]{1,0:T(8,128)S(1)} %get-tuple-element.19), channel_id=1, source_target_pairs={{0,6},{1,7},{2,0},{3,1},{4,2},{5,3},{6,4},{7,5},{8,14},{9,15},{10,... | collective-permute-start | bytes 49160 | tf_op jit(solution)/shard_map/ppermute | solution.py:197
  111.8 3.2 %collective-permute-start.6 = (f32[16,256]{1,0:T(8,128)S(1)}, f32[16,256]{1,0:T(8,128)S(1)}, u32[]{:S(2)}, u32[]{:S(2)}) collective-permute-start(f32[16,256]{1,0:T(8,128)S(1)} %get-tuple-element.20), channel_id=1, source_target_pairs={{0,7},{1,6},{2,1},{3,0},{4,3},{5,2},{6,5},{7,4},{8,15},{9,14},{10,... | collective-permute-start | bytes 49160 | tf_op jit(solution)/shard_map/ppermute | solution.py:197
  115.0 3.8 %collective-permute-start.9 = (f32[16,256]{1,0:T(8,128)S(1)}, f32[16,256]{1,0:T(8,128)S(1)}, u32[]{:S(2)}, u32[]{:S(2)}) collective-permute-start(f32[16,256]{1,0:T(8,128)S(1)} %add_add_fusion.refs_0_), channel_id=1, source_target_pairs={{0,192},{8,200},{16,208},{24,216},{32,224},{40,232},{48,240},{56,2... | collective-permute-start | bytes 49160 | tf_op jit(solution)/shard_map/ppermute | solution.py:202
  115.8 5.2 %collective-permute-start.8 = (f32[16,256]{1,0:T(8,128)S(1)}, f32[16,256]{1,0:T(8,128)S(1)}, u32[]{:S(2)}, u32[]{:S(2)}) collective-permute-start(f32[16,256]{1,0:T(8,128)S(1)} %add_add_fusion.refs_0_), channel_id=1, source_target_pairs={{0,128},{8,136},{16,144},{24,152},{32,160},{40,168},{48,176},{56,1... | collective-permute-start | bytes 49160 | tf_op jit(solution)/shard_map/ppermute | solution.py:202
  116.3 5.2 %collective-permute-start.7 = (f32[16,256]{1,0:T(8,128)S(1)}, f32[16,256]{1,0:T(8,128)S(1)}, u32[]{:S(2)}, u32[]{:S(2)}) collective-permute-start(f32[16,256]{1,0:T(8,128)S(1)} %add_add_fusion.refs_0_), channel_id=1, source_target_pairs={{0,64},{8,72},{16,80},{24,88},{32,96},{40,104},{48,112},{56,120},{... | collective-permute-start | bytes 49160 | tf_op jit(solution)/shard_map/ppermute | solution.py:202
  121.5 12.0 %collective-permute-start.16 = (f32[16,256]{1,0:T(8,128)S(1)}, f32[16,256]{1,0:T(8,128)S(1)}, u32[]{:S(2)}, u32[]{:S(2)}) collective-permute-start(f32[16,256]{1,0:T(8,128)S(1)} %sum_ring.2.refs_0_), channel_id=1, source_target_pairs={{0,56},{8,0},{16,8},{24,16},{32,24},{40,32},{48,40},{56,48},{64,12... | collective-permute-start | bytes 49160 | tf_op jit(solution)/shard_map/ppermute | solution.py:206
  123.9 12.5 %collective-permute-start.15 = (f32[16,256]{1,0:T(8,128)S(1)}, f32[16,256]{1,0:T(8,128)S(1)}, u32[]{:S(2)}, u32[]{:S(2)}) collective-permute-start(f32[16,256]{1,0:T(8,128)S(1)} %sum_ring.2.refs_0_), channel_id=1, source_target_pairs={{0,48},{8,56},{16,0},{24,8},{32,16},{40,24},{48,32},{56,40},{64,11... | collective-permute-start | bytes 49160 | tf_op jit(solution)/shard_map/ppermute | solution.py:206
  125.3 11.1 %collective-permute-start.14 = (f32[16,256]{1,0:T(8,128)S(1)}, f32[16,256]{1,0:T(8,128)S(1)}, u32[]{:S(2)}, u32[]{:S(2)}) collective-permute-start(f32[16,256]{1,0:T(8,128)S(1)} %sum_ring.2.refs_0_), channel_id=1, source_target_pairs={{0,40},{8,48},{16,56},{24,0},{32,8},{40,16},{48,24},{56,32},{64,10... | collective-permute-start | bytes 49160 | tf_op jit(solution)/shard_map/ppermute | solution.py:206
  129.5 7.7 %collective-permute-start.13 = (f32[16,256]{1,0:T(8,128)S(1)}, f32[16,256]{1,0:T(8,128)S(1)}, u32[]{:S(2)}, u32[]{:S(2)}) collective-permute-start(f32[16,256]{1,0:T(8,128)S(1)} %sum_ring.2.refs_0_), channel_id=1, source_target_pairs={{0,32},{8,40},{16,48},{24,56},{32,0},{40,8},{48,16},{56,24},{64,96... | collective-permute-start | bytes 49160 | tf_op jit(solution)/shard_map/ppermute | solution.py:206
  131.7 6.7 %collective-permute-start.12 = (f32[16,256]{1,0:T(8,128)S(1)}, f32[16,256]{1,0:T(8,128)S(1)}, u32[]{:S(2)}, u32[]{:S(2)}) collective-permute-start(f32[16,256]{1,0:T(8,128)S(1)} %sum_ring.2.refs_0_), channel_id=1, source_target_pairs={{0,24},{8,32},{16,40},{24,48},{32,56},{40,0},{48,8},{56,16},{64,88... | collective-permute-start | bytes 49160 | tf_op jit(solution)/shard_map/ppermute | solution.py:206
  133.4 5.8 %collective-permute-start.11 = (f32[16,256]{1,0:T(8,128)S(1)}, f32[16,256]{1,0:T(8,128)S(1)}, u32[]{:S(2)}, u32[]{:S(2)}) collective-permute-start(f32[16,256]{1,0:T(8,128)S(1)} %sum_ring.2.refs_0_), channel_id=1, source_target_pairs={{0,16},{8,24},{16,32},{24,40},{32,48},{40,56},{48,0},{56,8},{64,80... | collective-permute-start | bytes 49160 | tf_op jit(solution)/shard_map/ppermute | solution.py:206
  136.4 5.0 %collective-permute-start.10 = (f32[16,256]{1,0:T(8,128)S(1)}, f32[16,256]{1,0:T(8,128)S(1)}, u32[]{:S(2)}, u32[]{:S(2)}) collective-permute-start(f32[16,256]{1,0:T(8,128)S(1)} %sum_ring.2.refs_0_), channel_id=1, source_target_pairs={{0,8},{8,16},{16,24},{24,32},{32,40},{40,48},{48,56},{56,0},{64,72... | collective-permute-start | bytes 49160 | tf_op jit(solution)/shard_map/ppermute | solution.py:206

commit v2 on v1

v2 whole, which is shorter than its diff:
```python
import jax
import jax.numpy as jnp
from jax import lax
from jax.experimental import pallas as pl
from jax.experimental.pallas import tpu as pltpu
from jax.sharding import PartitionSpec as P

ALL = ("vir", "occ", "rep")
VIR = 32
GRP = 8
BLKS = 8
SLOTS = 12
LANE = 128
AHEAD = 6
MIB = 1 << 20


def slot_of_block(owners):
    ids = jnp.arange(owners.shape[0], dtype=jnp.int32)
    earlier = ids[None, :] < ids[:, None]
    same = owners[None, :] == owners[:, None]
    rank = jnp.sum(jnp.where(same & earlier, 1, 0), axis=1).astype(jnp.int32)
    return owners * SLOTS + rank


def spread_kernel(amp_ref, out_ref):
    for blk in range(BLKS):
        for chunk in range(32):
            part, quarter = chunk // 4, chunk % 4
            out_ref[pl.ds((quarter * GRP + part) * BLKS + blk, 8, stride=4 * GRP * BLKS), :] = (
                amp_ref[pl.ds(blk * 8, 8), pl.ds(chunk * LANE, LANE)]
            )


def spread(amp):
    return pl.pallas_call(
        spread_kernel,
        out_shape=jax.ShapeDtypeStruct((VIR * GRP * BLKS, LANE), jnp.float32),
        in_specs=[pl.BlockSpec(memory_space=pltpu.VMEM)],
        out_specs=pl.BlockSpec(memory_space=pltpu.VMEM),
        compiler_params=pltpu.CompilerParams(vmem_limit_bytes=8 * MIB),
        cost_estimate=pl.CostEstimate(flops=0, bytes_accessed=2 * MIB, transcendentals=0),
        name="spread",
    )(amp)


def route_kernel(slot_ref, got_ref, out_ref):
    def clear(i, carry):
        out_ref[pl.ds(i * SLOTS, SLOTS)] = jnp.zeros((SLOTS, GRP, LANE), jnp.float32)
        return carry

    lax.fori_loop(0, VIR, clear, 0)

    for source in range(VIR):
        for blk in range(BLKS):
            out_ref[slot_ref[source * BLKS + blk]] = got_ref[
                pl.ds(source * GRP * BLKS + blk, GRP, stride=BLKS), :
            ]


def route(slot, got):
    return pl.pallas_call(
        route_kernel,
        out_shape=jax.ShapeDtypeStruct((VIR * SLOTS, GRP, LANE), jnp.float32),
        in_specs=[
            pl.BlockSpec(memory_space=pltpu.SMEM),
            pl.BlockSpec(memory_space=pltpu.VMEM),
        ],
        out_specs=pl.BlockSpec(memory_space=pltpu.VMEM),
        compiler_params=pltpu.CompilerParams(vmem_limit_bytes=8 * MIB),
        cost_estimate=pl.CostEstimate(flops=0, bytes_accessed=3 * MIB, transcendentals=0),
        name="route",
    )(slot, got)


def split(value):
    high = value.astype(jnp.bfloat16)
    return high, (value - high.astype(jnp.float32)).astype(jnp.bfloat16)


def dot_nt(left, right):
    return lax.dot_general(
        left, right, (((1,), (1,)), ((), ())), preferred_element_type=jnp.float32
    )


def contract_kernel(
    place_ref, amp_ref, int_hbm, other_ref, near_ref, far_ref, held, acc, tiles, ordered, sems
):
    copies = [
        pltpu.make_async_copy(int_hbm.at[slot], held.at[slot], sems.at[slot])
        for slot in range(SLOTS)
    ]
    for copy in copies[:AHEAD]:
        copy.start()
    acc[...] = jnp.zeros_like(acc)
    for slot in range(SLOTS):
        rows = jnp.concatenate(
            [amp_ref[:, q, slot].reshape(64, LANE) for q in range(4)], axis=1
        )
        a_high, a_low = split(rows)
        copies[slot].wait()
        if slot + AHEAD < SLOTS:
            copies[slot + AHEAD].start()
        b_high, b_low = split(held[slot])
        both = dot_nt(jnp.concatenate([a_high, a_low], axis=0), b_high)
        acc[...] += both[:64] + both[64:] + dot_nt(a_high, b_low)
    for tile in range(4):
        tiles[tile] = acc[:, pl.ds(tile * LANE, LANE)]
    for tile in range(4):
        for group in range(GRP):
            ordered[tile // 2, pl.ds(group * 8, 8), pl.ds(tile % 2 * LANE, LANE)] = tiles[
                tile, pl.ds(group, 8, stride=GRP), :
            ]
    occ, rep = place_ref[0], place_ref[1]
    for k in range(4):
        rows = pl.ds(pl.multiple_of((occ ^ k) * 16, 16), 16)
        other_ref[pl.ds(k * 16, 16)] = ordered[1 - rep, rows, :]
        mine = far_ref if k >= 2 else near_ref
        mine[pl.ds(k % 2 * 16, 16)] = ordered[rep, rows, :]


def contract(place, amp, integrals):
    return pl.pallas_call(
        contract_kernel,
        out_shape=[
            jax.ShapeDtypeStruct((64, 256), jnp.float32),
            jax.ShapeDtypeStruct((32, 256), jnp.float32),
            jax.ShapeDtypeStruct((32, 256), jnp.float32),
        ],
        in_specs=[
            pl.BlockSpec(memory_space=pltpu.SMEM),
            pl.BlockSpec(memory_space=pltpu.VMEM),
            pl.BlockSpec(memory_space=pltpu.HBM),
        ],
        out_specs=[pl.BlockSpec(memory_space=pltpu.VMEM)] * 3,
        scratch_shapes=[
            pltpu.VMEM((SLOTS, 512, 512), jnp.float32),
            pltpu.VMEM((64, 512), jnp.float32),
            pltpu.VMEM((4, 64, LANE), jnp.float32),
            pltpu.VMEM((2, 64, 256), jnp.float32),
            pltpu.SemaphoreType.DMA((SLOTS,)),
        ],
        compiler_params=pltpu.CompilerParams(vmem_limit_bytes=56 * MIB),
        cost_estimate=pl.CostEstimate(
            flops=6 * 64 * 512 * 6144, bytes_accessed=14 * MIB, transcendentals=0
        ),
        name="contract",
    )(place, amp, integrals)


def flip(size, bit):
    return [(i, i ^ bit) for i in range(size)]


def on_device(amplitudes, integrals, block_owner):
    occ, rep = lax.axis_index("occ"), lax.axis_index("rep")
    slot = slot_of_block(block_owner)
    sent = spread(amplitudes.reshape(BLKS * 8, 4096))
    sent = sent.reshape(VIR * GRP, BLKS, LANE)
    got = lax.all_to_all(sent, ALL, split_axis=0, concat_axis=0, tiled=True)
    routed = route(slot, got.reshape(VIR * GRP * BLKS, LANE))
    owned = lax.all_to_all(
        routed.reshape(VIR, SLOTS * GRP, LANE), "vir", split_axis=0, concat_axis=0, tiled=True
    )
    other, near, far = contract(
        jnp.stack([occ, rep]), owned.reshape(8, 4, SLOTS, GRP, LANE), integrals
    )
    arrived = lax.ppermute(other, "rep", flip(2, 1))
    far = far + arrived[32:]
    near = near + arrived[:32]
    near = near + lax.ppermute(far, "occ", flip(4, 2))
    total = near[:16] + lax.ppermute(near[16:], "occ", flip(4, 1))
    for bit in (16, 8, 4, 2, 1):
        total = total + lax.ppermute(total, "vir", flip(VIR, bit))
    return total


def solution(mesh):
    in_specs = (P("vir", ("occ", "rep"), None), P("vir", None, ("occ", "rep")), P())
    out_specs = P("occ", "rep")
    return jax.shard_map(
        on_device, mesh=mesh, in_specs=in_specs, out_specs=out_specs, check_vma=False
    )
```

time: 143 us -> 143 us (level); the launches traced: 142 us -> 141 us
  starting transfers between devices: 44.9 us -> 28.1 us
  waiting for transfers between devices: 79.7 us -> 95 us
  local copies, waits for them, and re-layouts: 5.8 us -> 2.39 us
  other arithmetic: 0.27 us -> 2.94 us
    ppermute x17 -> x8, starting transfers between devices: 25.4 us -> 8.62 us  [the longest x5 5.52 us: on_device(): total = total + lax.ppermute(total, 'vir', flip(VIR, bit))]
    ppermute x17 -> x8, waiting for transfers between devices: 11.4 us -> 27.2 us  [the longest x5 19.5 us: on_device(): total = total + lax.ppermute(total, 'vir', flip(VIR, bit))]
    unnamed x6, local copies, waits for them, and re-layouts: 5.8 us -> 2.39 us
    add x1 -> x8, other arithmetic: 0.01 us -> 2.16 us  [the longest x1 0.77 us: on_device(): near = near + lax.ppermute(far, 'occ', flip(4, 2))]
    pallas_call x3 -> x1, Pallas kernels: 7.14 us -> 7.95 us  [contract(): pl.pallas_call(contract_kernel, out_shape=[jax.ShapeDtypeStruct((64, 256)...]
  transfers between devices with their start and end apart: 19 -> 10, of which waited for: 11 -> 10; matrix products, arithmetic and copies ran while one was open for 0% -> 1% of each run, Pallas kernels for 0% -> 0%
where the time goes in v2:
time: 143 us; the launch traced here: 141 us
  waiting for transfers between devices  95 us (66%)
  starting transfers between devices  28.1 us (20%)
  Pallas kernels  12 us (8%)
  other arithmetic  2.94 us (2%)
  local copies, waits for them, and re-layouts  2.39 us (2%)
    all_to_all x1, waiting for transfers between devices, on_device(): lax.all_to_all(routed.reshape(VIR, SLOTS * GRP, LANE), 'vir', split_axis=...  38.4 us
    all_to_all x1, waiting for transfers between devices, on_device(): got = lax.all_to_all(sent, ALL, split_axis=0, concat_axis=0, tiled=True)  29.4 us
    ppermute x5, waiting for transfers between devices, on_device(): total = total + lax.ppermute(total, 'vir', flip(VIR, bit))  19.5 us
    all_to_all x1, starting transfers between devices, on_device(): got = lax.all_to_all(sent, ALL, split_axis=0, concat_axis=0, tiled=True)  14.6 us
    pallas_call x1, Pallas kernels, contract(): pl.pallas_call(contract_kernel, out_shape=[jax.ShapeDtypeStruct((64, 256)...  7.95 us
    ppermute x5, starting transfers between devices, on_device(): total = total + lax.ppermute(total, 'vir', flip(VIR, bit))  5.52 us
    all_to_all x1, starting transfers between devices, on_device(): lax.all_to_all(routed.reshape(VIR, SLOTS * GRP, LANE), 'vir', split_axis=...  4.91 us
    ppermute x1, waiting for transfers between devices, on_device(): near = near + lax.ppermute(far, 'occ', flip(4, 2))  3.37 us
  transfers between devices with their start and end apart: 10, of which 10 were waited for; matrix products, arithmetic and copies ran while one was open for 1% of the time, Pallas kernels for 0%

profile of v2, /device:TPU:0, one launch (start us, length us, event | category | flops | bytes accessed | tf_op | source)
XLA Modules:
  0.0 140.5 jit_solution(10915025714204564714)
XLA Ops:
  0.0 0.0 copy-start
  0.0 1.2 copy-done
  1.2 1.9 %spread.1 = f32[2048,128]{1,0:T(8,128)} custom-call(f32[64,4096]{1,0:T(8,128)S(1)} %bitcast.8), custom_call_target="tpu_custom_call" | custom-call | bytes 2097152 | tf_op jit(solution)/shard_map/spread/pallas_call | solution.py:36
  3.2 0.0 copy-start.2
  3.2 14.6 %all-to-all-start = ((f32[256,8,128]{2,1,0:T(8,128)}), f32[256,8,128]{2,1,0:T(8,128)S(1)}, u32[]{:S(2)}, u32[]{:S(2)}) async-start(f32[256,8,128]{2,1,0:T(8,128)} %bitcast.3), calls=%async_computation | async-start | bytes 2097152 | tf_op jit(solution)/shard_map/all_to_all | solution.py:161
  17.7 0.0 copy-done.2
  17.7 0.2 select_reduce_fusion
  17.9 29.4 %all-to-all-done = f32[256,8,128]{2,1,0:T(8,128)S(1)} async-done(((f32[256,8,128]{2,1,0:T(8,128)}), f32[256,8,128]{2,1,0:T(8,128)S(1)}, u32[]{:S(2)}, u32[]{:S(2)}) %all-to-all-start) | async-done | bytes 1048608 | tf_op jit(solution)/shard_map/all_to_all | solution.py:161
  47.3 2.1 %route.1 = f32[384,8,128]{2,1,0:T(8,128)} custom-call(s32[256]{0:T(256)S(1)} %multiply_add_fusion.slot_ref, f32[2048,128]{1,0:T(8,128)S(1)} %bitcast.7), custom_call_target="tpu_custom_call" | custom-call | bytes 3145728 | tf_op jit(solution)/shard_map/route/pallas_call | solution.py:62
  49.4 4.9 %all-to-all-start.1 = ((f32[32,96,128]{2,1,0:T(8,128)}), f32[32,96,128]{2,1,0:T(8,128)S(1)}, u32[]{:S(2)}, u32[]{:S(2)}) async-start(f32[32,96,128]{2,1,0:T(8,128)} %bitcast.5), calls=%async_computation.1 | async-start | bytes 3145728 | tf_op jit(solution)/shard_map/all_to_all | solution.py:163
  54.4 0.6 pad_add_fusion.place_ref
  55.0 38.4 %all-to-all-done.1 = f32[32,96,128]{2,1,0:T(8,128)S(1)} async-done(((f32[32,96,128]{2,1,0:T(8,128)}), f32[32,96,128]{2,1,0:T(8,128)S(1)}, u32[]{:S(2)}, u32[]{:S(2)}) %all-to-all-start.1) | async-done | bytes 1572896 | tf_op jit(solution)/shard_map/all_to_all | solution.py:163
  93.4 0.0 copy-start.1
  93.4 1.2 copy-done.1
  94.6 8.0 %contract.1 = (f32[64,256]{1,0:T(8,128)}, f32[32,256]{1,0:T(8,128)}, f32[32,256]{1,0:T(8,128)}) custom-call(s32[2]{0:T(128)} %pad_add_fusion.place_ref, f32[8,4,12,8,128]{4,3,2,1,0:T(8,128)} %bitcast.9, f32[12,512,512]{2,1,0:T(8,128)} %int_hbm.1), custom_call_target="tpu_custom_call" | custom-call | flops 1207959552 | bytes 14680064 | tf_op jit(solution)/shard_map/contract/pallas_call | solution.py:124
  102.5 0.1 collective-permute-start
  102.6 1.5 %collective-permute-done = f32[64,256]{1,0:T(8,128)S(1)} collective-permute-done((f32[64,256]{1,0:T(8,128)}, f32[64,256]{1,0:T(8,128)S(1)}, u32[]{:S(2)}, u32[]{:S(2)}) %collective-permute-start) | collective-permute-done | bytes 65568 | tf_op jit(solution)/shard_map/ppermute | solution.py:169
  104.1 0.8 slice_add_fusion
  104.8 2.1 %collective-permute-start.1 = (f32[32,256]{1,0:T(8,128)S(1)}, f32[32,256]{1,0:T(8,128)S(1)}, u32[]{:S(2)}, u32[]{:S(2)}) collective-permute-start(f32[32,256]{1,0:T(8,128)S(1)} %slice_add_fusion), channel_id=1, source_target_pairs={{0,4},{2,6},{4,0},{6,2},{1,5},{3,7},{5,1},{7,3},{8,12},{10,14},{12... | collective-permute-start | bytes 98312 | tf_op jit(solution)/shard_map/ppermute | solution.py:172
  106.9 3.4 %collective-permute-done.1 = f32[32,256]{1,0:T(8,128)S(1)} collective-permute-done((f32[32,256]{1,0:T(8,128)S(1)}, f32[32,256]{1,0:T(8,128)S(1)}, u32[]{:S(2)}, u32[]{:S(2)}) %collective-permute-start.1) | collective-permute-done | bytes 32800 | tf_op jit(solution)/shard_map/ppermute | solution.py:172
  110.3 0.8 fusion.1
  111.0 1.0 collective-permute-start.2
  112.0 2.9 %collective-permute-done.2 = f32[16,256]{1,0:T(8,128)S(1)} collective-permute-done((f32[16,256]{1,0:T(8,128)S(1)}, f32[16,256]{1,0:T(8,128)S(1)}, u32[]{:S(2)}, u32[]{:S(2)}) %collective-permute-start.2) | collective-permute-done | bytes 16416 | tf_op jit(solution)/shard_map/ppermute | solution.py:173
  114.9 0.8 collective-permute-start.3
  115.6 4.5 %collective-permute-done.3 = f32[16,256]{1,0:T(8,128)S(1)} collective-permute-done((f32[16,256]{1,0:T(8,128)S(1)}, f32[16,256]{1,0:T(8,128)S(1)}, u32[]{:S(2)}, u32[]{:S(2)}) %collective-permute-start.3) | collective-permute-done | bytes 16416 | tf_op jit(solution)/shard_map/ppermute | solution.py:175
  120.1 0.0 collective-permute-start.4
  120.1 3.7 %collective-permute-done.4 = f32[16,256]{1,0:T(8,128)S(1)} collective-permute-done((f32[16,256]{1,0:T(8,128)S(1)}, f32[16,256]{1,0:T(8,128)S(1)}, u32[]{:S(2)}, u32[]{:S(2)}) %collective-permute-start.4) | collective-permute-done | bytes 16416 | tf_op jit(solution)/shard_map/ppermute | solution.py:175
  123.9 1.6 %collective-permute-start.5 = (f32[16,256]{1,0:T(8,128)S(1)}, f32[16,256]{1,0:T(8,128)S(1)}, u32[]{:S(2)}, u32[]{:S(2)}) collective-permute-start(f32[16,256]{1,0:T(8,128)S(1)} %add.36), channel_id=1, source_target_pairs={{0,32},{8,40},{16,48},{24,56},{32,0},{40,8},{48,16},{56,24},{64,96... | collective-permute-start | bytes 49160 | tf_op jit(solution)/shard_map/ppermute | solution.py:175
  125.4 6.1 %collective-permute-done.5 = f32[16,256]{1,0:T(8,128)S(1)} collective-permute-done((f32[16,256]{1,0:T(8,128)S(1)}, f32[16,256]{1,0:T(8,128)S(1)}, u32[]{:S(2)}, u32[]{:S(2)}) %collective-permute-start.5) | collective-permute-done | bytes 16416 | tf_op jit(solution)/shard_map/ppermute | solution.py:175
  131.6 1.3 collective-permute-start.6
  132.9 3.3 %collective-permute-done.6 = f32[16,256]{1,0:T(8,128)S(1)} collective-permute-done((f32[16,256]{1,0:T(8,128)S(1)}, f32[16,256]{1,0:T(8,128)S(1)}, u32[]{:S(2)}, u32[]{:S(2)}) %collective-permute-start.6) | collective-permute-done | bytes 16416 | tf_op jit(solution)/shard_map/ppermute | solution.py:175
  136.2 1.8 %collective-permute-start.7 = (f32[16,256]{1,0:T(8,128)S(1)}, f32[16,256]{1,0:T(8,128)S(1)}, u32[]{:S(2)}, u32[]{:S(2)}) collective-permute-start(f32[16,256]{1,0:T(8,128)S(1)} %add.38), channel_id=1, source_target_pairs={{0,8},{8,0},{16,24},{24,16},{32,40},{40,32},{48,56},{56,48},{64,72... | collective-permute-start | bytes 49160 | tf_op jit(solution)/shard_map/ppermute | solution.py:175
  138.0 1.9 %collective-permute-done.7 = f32[16,256]{1,0:T(8,128)S(1)} collective-permute-done((f32[16,256]{1,0:T(8,128)S(1)}, f32[16,256]{1,0:T(8,128)S(1)}, u32[]{:S(2)}, u32[]{:S(2)}) %collective-permute-start.7) | collective-permute-done | bytes 16416 | tf_op jit(solution)/shard_map/ppermute | solution.py:175
  139.9 0.6 add.39
  (7 shorter events, 0.0 us)
Async XLA Ops:
  0.0 1.2 copy-start
  3.2 14.6 %copy-start.2 = (s32[256]{0:T(256)S(1)}, s32[256]{0:T(256)}, u32[]{:S(2)}) copy-start(s32[256]{0:T(256)} %param.5) | copy-start | bytes 3076
  3.2 44.2 %all-to-all-start = ((f32[256,8,128]{2,1,0:T(8,128)}), f32[256,8,128]{2,1,0:T(8,128)S(1)}, u32[]{:S(2)}, u32[]{:S(2)}) async-start(f32[256,8,128]{2,1,0:T(8,128)} %bitcast.3), calls=%async_computation | async-start | bytes 2097152 | tf_op jit(solution)/shard_map/all_to_all | solution.py:161
  49.4 44.0 %all-to-all-start.1 = ((f32[32,96,128]{2,1,0:T(8,128)}), f32[32,96,128]{2,1,0:T(8,128)S(1)}, u32[]{:S(2)}, u32[]{:S(2)}) async-start(f32[32,96,128]{2,1,0:T(8,128)} %bitcast.5), calls=%async_computation.1 | async-start | bytes 3145728 | tf_op jit(solution)/shard_map/all_to_all | solution.py:163
  93.4 1.2 copy-start.1
  102.5 1.6 %collective-permute-start = (f32[64,256]{1,0:T(8,128)}, f32[64,256]{1,0:T(8,128)S(1)}, u32[]{:S(2)}, u32[]{:S(2)}) collective-permute-start(f32[64,256]{1,0:T(8,128)} %get-tuple-element.9), channel_id=1, source_target_pairs={{0,1},{1,0},{2,3},{3,2},{4,5},{5,4},{6,7},{7,6},{8,9},{9,8},{10,11... | collective-permute-start | bytes 196616 | tf_op jit(solution)/shard_map/ppermute | solution.py:169
  104.8 5.4 %collective-permute-start.1 = (f32[32,256]{1,0:T(8,128)S(1)}, f32[32,256]{1,0:T(8,128)S(1)}, u32[]{:S(2)}, u32[]{:S(2)}) collective-permute-start(f32[32,256]{1,0:T(8,128)S(1)} %slice_add_fusion), channel_id=1, source_target_pairs={{0,4},{2,6},{4,0},{6,2},{1,5},{3,7},{5,1},{7,3},{8,12},{10,14},{12... | collective-permute-start | bytes 98312 | tf_op jit(solution)/shard_map/ppermute | solution.py:172
  111.0 3.8 %collective-permute-start.2 = (f32[16,256]{1,0:T(8,128)S(1)}, f32[16,256]{1,0:T(8,128)S(1)}, u32[]{:S(2)}, u32[]{:S(2)}) collective-permute-start(f32[16,256]{1,0:T(8,128)S(1)} %slice.19), channel_id=1, source_target_pairs={{0,2},{2,0},{4,6},{6,4},{1,3},{3,1},{5,7},{7,5},{8,10},{10,8},{12,... | collective-permute-start | bytes 49160 | tf_op jit(solution)/shard_map/ppermute | solution.py:173
  114.9 5.2 %collective-permute-start.3 = (f32[16,256]{1,0:T(8,128)S(1)}, f32[16,256]{1,0:T(8,128)S(1)}, u32[]{:S(2)}, u32[]{:S(2)}) collective-permute-start(f32[16,256]{1,0:T(8,128)S(1)} %slice_add_fusion.2), channel_id=1, source_target_pairs={{0,128},{8,136},{16,144},{24,152},{32,160},{40,168},{48,176},{56,1... | collective-permute-start | bytes 49160 | tf_op jit(solution)/shard_map/ppermute | solution.py:175
  120.1 3.7 %collective-permute-start.4 = (f32[16,256]{1,0:T(8,128)S(1)}, f32[16,256]{1,0:T(8,128)S(1)}, u32[]{:S(2)}, u32[]{:S(2)}) collective-permute-start(f32[16,256]{1,0:T(8,128)S(1)} %add.35), channel_id=1, source_target_pairs={{0,64},{8,72},{16,80},{24,88},{32,96},{40,104},{48,112},{56,120},{... | collective-permute-start | bytes 49160 | tf_op jit(solution)/shard_map/ppermute | solution.py:175
  123.9 7.7 %collective-permute-start.5 = (f32[16,256]{1,0:T(8,128)S(1)}, f32[16,256]{1,0:T(8,128)S(1)}, u32[]{:S(2)}, u32[]{:S(2)}) collective-permute-start(f32[16,256]{1,0:T(8,128)S(1)} %add.36), channel_id=1, source_target_pairs={{0,32},{8,40},{16,48},{24,56},{32,0},{40,8},{48,16},{56,24},{64,96... | collective-permute-start | bytes 49160 | tf_op jit(solution)/shard_map/ppermute | solution.py:175
  131.6 4.6 %collective-permute-start.6 = (f32[16,256]{1,0:T(8,128)S(1)}, f32[16,256]{1,0:T(8,128)S(1)}, u32[]{:S(2)}, u32[]{:S(2)}) collective-permute-start(f32[16,256]{1,0:T(8,128)S(1)} %add.37), channel_id=1, source_target_pairs={{0,16},{8,24},{16,0},{24,8},{32,48},{40,56},{48,32},{56,40},{64,80... | collective-permute-start | bytes 49160 | tf_op jit(solution)/shard_map/ppermute | solution.py:175
  136.2 3.7 %collective-permute-start.7 = (f32[16,256]{1,0:T(8,128)S(1)}, f32[16,256]{1,0:T(8,128)S(1)}, u32[]{:S(2)}, u32[]{:S(2)}) collective-permute-start(f32[16,256]{1,0:T(8,128)S(1)} %add.38), channel_id=1, source_target_pairs={{0,8},{8,0},{16,24},{24,16},{32,40},{40,32},{48,56},{56,48},{64,72... | collective-permute-start | bytes 49160 | tf_op jit(solution)/shard_map/ppermute | solution.py:175

commit v3 on v2

--- a/solution.py
+++ b/solution.py
@@ -84,9 +84,7 @@
     )
 
 
-def contract_kernel(
-    place_ref, amp_ref, int_hbm, other_ref, near_ref, far_ref, held, acc, tiles, ordered, sems
-):
+def contract_kernel(amp_ref, int_hbm, out_ref, held, acc, tiles, ordered, sems):
     copies = [
         pltpu.make_async_copy(int_hbm.at[slot], held.at[slot], sems.at[slot])
         for slot in range(SLOTS)
@@ -112,28 +110,19 @@
             ordered[tile // 2, pl.ds(group * 8, 8), pl.ds(tile % 2 * LANE, LANE)] = tiles[
                 tile, pl.ds(group, 8, stride=GRP), :
             ]
-    occ, rep = place_ref[0], place_ref[1]
-    for k in range(4):
-        rows = pl.ds(pl.multiple_of((occ ^ k) * 16, 16), 16)
-        other_ref[pl.ds(k * 16, 16)] = ordered[1 - rep, rows, :]
-        mine = far_ref if k >= 2 else near_ref
-        mine[pl.ds(k % 2 * 16, 16)] = ordered[rep, rows, :]
+    for part in range(GRP):
+        out_ref[part] = ordered[part % 2, pl.ds(part // 2 * 16, 16), :]
 
 
-def contract(place, amp, integrals):
+def contract(amp, integrals):
     return pl.pallas_call(
         contract_kernel,
-        out_shape=[
-            jax.ShapeDtypeStruct((64, 256), jnp.float32),
-            jax.ShapeDtypeStruct((32, 256), jnp.float32),
-            jax.ShapeDtypeStruct((32, 256), jnp.float32),
-        ],
+        out_shape=jax.ShapeDtypeStruct((GRP, 16, 256), jnp.float32),
         in_specs=[
-            pl.BlockSpec(memory_space=pltpu.SMEM),
             pl.BlockSpec(memory_space=pltpu.VMEM),
             pl.BlockSpec(memory_space=pltpu.HBM),
         ],
-        out_specs=[pl.BlockSpec(memory_space=pltpu.VMEM)] * 3,
+        out_specs=pl.BlockSpec(memory_space=pltpu.VMEM),
         scratch_shapes=[
             pltpu.VMEM((SLOTS, 512, 512), jnp.float32),
             pltpu.VMEM((64, 512), jnp.float32),
@@ -141,20 +130,40 @@
             pltpu.VMEM((2, 64, 256), jnp.float32),
             pltpu.SemaphoreType.DMA((SLOTS,)),
         ],
-        compiler_params=pltpu.CompilerParams(vmem_limit_bytes=56 * MIB),
+        compiler_params=pltpu.CompilerParams(vmem_limit_bytes=50 * MIB),
         cost_estimate=pl.CostEstimate(
             flops=6 * 64 * 512 * 6144, bytes_accessed=14 * MIB, transcendentals=0
         ),
         name="contract",
-    )(place, amp, integrals)
+    )(amp, integrals)
 
 
-def flip(size, bit):
-    return [(i, i ^ bit) for i in range(size)]
+def sum_x_kernel(place_ref, *refs):
+    ins, out_ref, held = refs[:4], refs[4], refs[5]
+    for k in range(4):
+        held[lax.rem(place_ref[0] + 4 - k, 4)] = ins[k][...]
+    out_ref[...] = (held[0] + held[1]) + (held[2] + held[3])
+
+
+def sum_x(place, pieces):
+    return pl.pallas_call(
+        sum_x_kernel,
+        out_shape=jax.ShapeDtypeStruct((16, 256), jnp.float32),
+        in_specs=[pl.BlockSpec(memory_space=pltpu.SMEM)]
+        + [pl.BlockSpec(memory_space=pltpu.VMEM)] * 4,
+        out_specs=pl.BlockSpec(memory_space=pltpu.VMEM),
+        scratch_shapes=[pltpu.VMEM((4, 16, 256), jnp.float32)],
+        compiler_params=pltpu.CompilerParams(vmem_limit_bytes=4 * MIB),
+        name="sum_x",
+    )(place, *pieces)
+
+
+def x_shift(k):
+    return [(x * 8 + z, (x + k) % 4 * 8 + z) for x in range(4) for z in range(8)]
 
 
 def on_device(amplitudes, integrals, block_owner):
-    occ, rep = lax.axis_index("occ"), lax.axis_index("rep")
+    x_place = (lax.axis_index("vir") // 8)[None]
     slot = slot_of_block(block_owner)
     sent = spread(amplitudes.reshape(BLKS * 8, 4096))
     sent = sent.reshape(VIR * GRP, BLKS, LANE)
@@ -163,17 +172,16 @@
     owned = lax.all_to_all(
         routed.reshape(VIR, SLOTS * GRP, LANE), "vir", split_axis=0, concat_axis=0, tiled=True
     )
-    other, near, far = contract(
-        jnp.stack([occ, rep]), owned.reshape(8, 4, SLOTS, GRP, LANE), integrals
+    pieces = contract(owned.reshape(8, 4, SLOTS, GRP, LANE), integrals)
+    total = jnp.sum(lax.all_to_all(pieces, ("occ", "rep"), 0, 0, tiled=True), axis=0)
+    total = sum_x(
+        x_place, [total] + [lax.ppermute(total, "vir", x_shift(k)) for k in range(1, 4)]
     )
-    arrived = lax.ppermute(other, "rep", flip(2, 1))
-    far = far + arrived[32:]
-    near = near + arrived[:32]
-    near = near + lax.ppermute(far, "occ", flip(4, 2))
-    total = near[:16] + lax.ppermute(near[16:], "occ", flip(4, 1))
-    for bit in (16, 8, 4, 2, 1):
-        total = total + lax.ppermute(total, "vir", flip(VIR, bit))
-    return total
+    every_z = [[x * 8 + z for z in range(8)] for x in range(4)]
+    copies = jnp.broadcast_to(total[None], (8, 16, 256))
+    return jnp.sum(
+        lax.all_to_all(copies, "vir", 0, 0, axis_index_groups=every_z, tiled=True), axis=0
+    )
 
 
 def solution(mesh):

time: 143 us -> 129 us (0.902); the launches traced: 141 us -> 128 us
  blocking collectives: 0 us -> 66.6 us
  waiting for transfers between devices: 95 us -> 33.9 us
  starting transfers between devices: 28.1 us -> 16.9 us
  Pallas kernels: 12 us -> 8.81 us
  other arithmetic: 2.94 us -> 0.82 us
    all_to_all x0 -> x3, blocking collectives: none -> 66.6 us  [the longest x1 44.5 us: on_device(): lax.all_to_all(routed.reshape(VIR, SLOTS * GRP, LANE), 'vir', split_axis=...]
    all_to_all x1 -> x0, waiting for transfers between devices: 38.4 us -> none  [on_device(): lax.all_to_all(routed.reshape(VIR, SLOTS * GRP, LANE), 'vir', split_axis=...]
    ppermute x8 -> x3, waiting for transfers between devices: 27.2 us -> 4.48 us  [on_device(): lax.ppermute(total, 'vir', x_shift(k))]
    ppermute x8 -> x3, starting transfers between devices: 8.62 us -> 2.35 us  [on_device(): lax.ppermute(total, 'vir', x_shift(k))]
    all_to_all x1 -> x0, starting transfers between devices: 4.91 us -> none  [on_device(): lax.all_to_all(routed.reshape(VIR, SLOTS * GRP, LANE), 'vir', split_axis=...]
    add x8 -> x0, other arithmetic: 2.16 us -> none  [the longest x1 0.77 us: on_device(): near = near + lax.ppermute(far, 'occ', flip(4, 2))]
    pallas_call x1 -> x2, Pallas kernels: 7.95 us -> 5.9 us  [the longest x1 5.88 us: contract(): pl.pallas_call(contract_kernel, out_shape=jax.ShapeDtypeStruct((GRP, 16,...]
  transfers between devices with their start and end apart: 10 -> 4, of which waited for: 10 -> 4; matrix products, arithmetic and copies ran while one was open for 1% -> 0% of each run, Pallas kernels for 0% -> 0%
where the time goes in v3:
time: 129 us; the launch traced here: 128 us
  blocking collectives  66.6 us (52%)
  waiting for transfers between devices  33.9 us (26%)
  starting transfers between devices  16.9 us (13%)
  Pallas kernels  8.81 us (7%)
    all_to_all x1, blocking collectives, on_device(): lax.all_to_all(routed.reshape(VIR, SLOTS * GRP, LANE), 'vir', split_axis=...  44.5 us
    all_to_all x1, waiting for transfers between devices, on_device(): got = lax.all_to_all(sent, ALL, split_axis=0, concat_axis=0, tiled=True)  29.4 us
    all_to_all x1, starting transfers between devices, on_device(): got = lax.all_to_all(sent, ALL, split_axis=0, concat_axis=0, tiled=True)  14.6 us
    all_to_all x1, blocking collectives, on_device(): lax.all_to_all(copies, 'vir', 0, 0, axis_index_groups=every_z, tiled=True)  13.6 us
    all_to_all x1, blocking collectives, on_device(): lax.all_to_all(pieces, ('occ', 'rep'), 0, 0, tiled=True)  8.52 us
    pallas_call x1, Pallas kernels, contract(): pl.pallas_call(contract_kernel, out_shape=jax.ShapeDtypeStruct((GRP, 16,...  5.88 us
    ppermute x3, waiting for transfers between devices, on_device(): lax.ppermute(total, 'vir', x_shift(k))  4.48 us
  transfers between devices with their start and end apart: 4, of which 4 were waited for; matrix products, arithmetic and copies ran while one was open for 0% of the time, Pallas kernels for 0%

profile of v3, /device:TPU:0, one launch (start us, length us, event | category | flops | bytes accessed | tf_op | source)
XLA Modules:
  0.0 128.3 jit_solution(4980167232617762138)
XLA Ops:
  0.0 0.0 copy-start
  0.0 1.2 copy-done
  1.2 2.0 %spread.1 = f32[2048,128]{1,0:T(8,128)} custom-call(f32[64,4096]{1,0:T(8,128)S(1)} %bitcast.9), custom_call_target="tpu_custom_call" | custom-call | bytes 2097152 | tf_op jit(solution)/shard_map/spread/pallas_call | solution.py:36
  3.2 0.0 copy-start.1
  3.2 14.6 %all-to-all-start = ((f32[256,8,128]{2,1,0:T(8,128)}), f32[256,8,128]{2,1,0:T(8,128)S(1)}, u32[]{:S(2)}, u32[]{:S(2)}) async-start(f32[256,8,128]{2,1,0:T(8,128)} %bitcast.2), calls=%async_computation | async-start | bytes 2097152 | tf_op jit(solution)/shard_map/all_to_all | solution.py:170
  17.8 0.0 copy-done.1
  17.8 0.2 select_reduce_fusion
  18.0 29.4 %all-to-all-done = f32[256,8,128]{2,1,0:T(8,128)S(1)} async-done(((f32[256,8,128]{2,1,0:T(8,128)}), f32[256,8,128]{2,1,0:T(8,128)S(1)}, u32[]{:S(2)}, u32[]{:S(2)}) %all-to-all-start) | async-done | bytes 1048608 | tf_op jit(solution)/shard_map/all_to_all | solution.py:170
  47.3 1.0 route.1
  48.3 44.5 %all_to_all.20 = f32[32,96,128]{2,1,0:T(8,128)S(1)} all-to-all(f32[32,96,128]{2,1,0:T(8,128)S(1)} %bitcast.6), channel_id=1, replica_groups=mesh['vir'=32,'occ'=4,'rep'=2] {'vir'}, dimensions={0} | all-to-all | bytes 3145728 | tf_op jit(solution)/shard_map/all_to_all | solution.py:172
  92.8 5.9 %contract.1 = f32[8,16,256]{2,1,0:T(8,128)S(1)} custom-call(f32[8,4,12,8,128]{4,3,2,1,0:T(8,128)S(1)} %bitcast.7, f32[12,512,512]{2,1,0:T(8,128)} %int_hbm.1), custom_call_target="tpu_custom_call" | custom-call | flops 1207959552 | bytes 14680064 | tf_op jit(solution)/shard_map/contract/pallas_call | solution.py:118
  98.7 8.5 %all_to_all.21 = f32[8,16,256]{2,1,0:T(8,128)S(1)} all-to-all(f32[8,16,256]{2,1,0:T(8,128)S(1)} %contract.1), channel_id=1, replica_groups=mesh['vir'=32,'occ'=4,'rep'=2] {'occ','rep'}, dimensions={0} | all-to-all | bytes 262144 | tf_op jit(solution)/shard_map/all_to_all | solution.py:176
  107.3 0.9 collective-permute-start.2
  108.1 1.0 collective-permute-start.1
  109.1 0.5 collective-permute-start
  109.6 1.5 %collective-permute-done.2.refs_3_ = f32[16,256]{1,0:T(8,128)S(1)} collective-permute-done((f32[16,256]{1,0:T(8,128)S(1)}, f32[16,256]{1,0:T(8,128)S(1)}, u32[]{:S(2)}, u32[]{:S(2)}) %collective-permute-start.2) | collective-permute-done | bytes 16416 | tf_op jit(solution)/shard_map/ppermute | solution.py:178
  111.1 2.4 %collective-permute-done.1.refs_2_ = f32[16,256]{1,0:T(8,128)S(1)} collective-permute-done((f32[16,256]{1,0:T(8,128)S(1)}, f32[16,256]{1,0:T(8,128)S(1)}, u32[]{:S(2)}, u32[]{:S(2)}) %collective-permute-start.1) | collective-permute-done | bytes 16416 | tf_op jit(solution)/shard_map/ppermute | solution.py:178
  113.5 0.6 collective-permute-done.refs_1_
  114.1 13.6 %all_to_all.22 = f32[8,16,256]{2,1,0:T(8,128)S(1)} all-to-all(f32[8,16,256]{2,1,0:T(8,128)S(1)} %broadcast_in_dim.24), channel_id=1, replica_groups={{0,8,16,24,32,40,48,56},{64,72,80,88,96,104,112,120},{128,136,144,152,1..., dimensions={0} | all-to-all | bytes 262144 | tf_op jit(solution)/shard_map/all_to_all | solution.py:183
  127.7 0.6 reduce_sum.29
  (4 shorter events, 0.0 us)
Async XLA Ops:
  0.0 1.2 copy-start
  3.2 14.6 %copy-start.1 = (s32[256]{0:T(256)S(1)}, s32[256]{0:T(256)}, u32[]{:S(2)}) copy-start(s32[256]{0:T(256)} %param.5) | copy-start | bytes 3076
  3.2 44.2 %all-to-all-start = ((f32[256,8,128]{2,1,0:T(8,128)}), f32[256,8,128]{2,1,0:T(8,128)S(1)}, u32[]{:S(2)}, u32[]{:S(2)}) async-start(f32[256,8,128]{2,1,0:T(8,128)} %bitcast.2), calls=%async_computation | async-start | bytes 2097152 | tf_op jit(solution)/shard_map/all_to_all | solution.py:170
  107.3 3.8 %collective-permute-start.2 = (f32[16,256]{1,0:T(8,128)S(1)}, f32[16,256]{1,0:T(8,128)S(1)}, u32[]{:S(2)}, u32[]{:S(2)}) collective-permute-start(f32[16,256]{1,0:T(8,128)S(1)} %reduce_sum.28.refs_0_), channel_id=1, source_target_pairs={{0,192},{8,200},{16,208},{24,216},{32,224},{40,232},{48,240},{56,2... | collective-permute-start | bytes 49160 | tf_op jit(solution)/shard_map/ppermute | solution.py:178
  108.1 5.4 %collective-permute-start.1 = (f32[16,256]{1,0:T(8,128)S(1)}, f32[16,256]{1,0:T(8,128)S(1)}, u32[]{:S(2)}, u32[]{:S(2)}) collective-permute-start(f32[16,256]{1,0:T(8,128)S(1)} %reduce_sum.28.refs_0_), channel_id=1, source_target_pairs={{0,128},{8,136},{16,144},{24,152},{32,160},{40,168},{48,176},{56,1... | collective-permute-start | bytes 49160 | tf_op jit(solution)/shard_map/ppermute | solution.py:178
  109.1 4.9 %collective-permute-start = (f32[16,256]{1,0:T(8,128)S(1)}, f32[16,256]{1,0:T(8,128)S(1)}, u32[]{:S(2)}, u32[]{:S(2)}) collective-permute-start(f32[16,256]{1,0:T(8,128)S(1)} %reduce_sum.28.refs_0_), channel_id=1, source_target_pairs={{0,64},{8,72},{16,80},{24,88},{32,96},{40,104},{48,112},{56,120},{... | collective-permute-start | bytes 49160 | tf_op jit(solution)/shard_map/ppermute | solution.py:178

commit v4 on v3

--- a/solution.py
+++ b/solution.py
@@ -3,9 +3,9 @@
 from jax import lax
 from jax.experimental import pallas as pl
 from jax.experimental.pallas import tpu as pltpu
+from jax.sharding import Mesh
 from jax.sharding import PartitionSpec as P
 
-ALL = ("vir", "occ", "rep")
 VIR = 32
 GRP = 8
 BLKS = 8
@@ -20,16 +20,17 @@
     earlier = ids[None, :] < ids[:, None]
     same = owners[None, :] == owners[:, None]
     rank = jnp.sum(jnp.where(same & earlier, 1, 0), axis=1).astype(jnp.int32)
-    return owners * SLOTS + rank
+    return (owners % 8 * 4 + owners // 8) * SLOTS + rank
 
 
 def spread_kernel(amp_ref, out_ref):
     for blk in range(BLKS):
         for chunk in range(32):
             part, quarter = chunk // 4, chunk % 4
-            out_ref[pl.ds((quarter * GRP + part) * BLKS + blk, 8, stride=4 * GRP * BLKS), :] = (
-                amp_ref[pl.ds(blk * 8, 8), pl.ds(chunk * LANE, LANE)]
-            )
+            first = (part * VIR + quarter) * BLKS + blk
+            out_ref[pl.ds(first, 8, stride=4 * BLKS), :] = amp_ref[
+                pl.ds(blk * 8, 8), pl.ds(chunk * LANE, LANE)
+            ]
 
 
 def spread(amp):
@@ -53,8 +54,9 @@
 
     for source in range(VIR):
         for blk in range(BLKS):
-            out_ref[slot_ref[source * BLKS + blk]] = got_ref[
-                pl.ds(source * GRP * BLKS + blk, GRP, stride=BLKS), :
+            vir = source % 4 * 8 + source // 4
+            out_ref[slot_ref[vir * BLKS + blk]] = got_ref[
+                pl.ds(source * BLKS + blk, GRP, stride=VIR * BLKS), :
             ]
 
 
@@ -159,34 +161,33 @@
 
 
 def x_shift(k):
-    return [(x * 8 + z, (x + k) % 4 * 8 + z) for x in range(4) for z in range(8)]
+    return [(x, (x + k) % 4) for x in range(4)]
 
 
 def on_device(amplitudes, integrals, block_owner):
-    x_place = (lax.axis_index("vir") // 8)[None]
+    x_place = lax.axis_index("x")[None]
     slot = slot_of_block(block_owner)
     sent = spread(amplitudes.reshape(BLKS * 8, 4096))
     sent = sent.reshape(VIR * GRP, BLKS, LANE)
-    got = lax.all_to_all(sent, ALL, split_axis=0, concat_axis=0, tiled=True)
+    got = lax.all_to_all(sent, ("occ", "rep", "z", "x"), 0, 0, tiled=True)
     routed = route(slot, got.reshape(VIR * GRP * BLKS, LANE))
-    owned = lax.all_to_all(
-        routed.reshape(VIR, SLOTS * GRP, LANE), "vir", split_axis=0, concat_axis=0, tiled=True
-    )
+    owned = lax.all_to_all(routed.reshape(VIR, SLOTS * GRP, LANE), ("z", "x"), 0, 0, tiled=True)
     pieces = contract(owned.reshape(8, 4, SLOTS, GRP, LANE), integrals)
     total = jnp.sum(lax.all_to_all(pieces, ("occ", "rep"), 0, 0, tiled=True), axis=0)
     total = sum_x(
-        x_place, [total] + [lax.ppermute(total, "vir", x_shift(k)) for k in range(1, 4)]
+        x_place, [total] + [lax.ppermute(total, "x", x_shift(k)) for k in range(1, 4)]
     )
-    every_z = [[x * 8 + z for z in range(8)] for x in range(4)]
     copies = jnp.broadcast_to(total[None], (8, 16, 256))
-    return jnp.sum(
-        lax.all_to_all(copies, "vir", 0, 0, axis_index_groups=every_z, tiled=True), axis=0
-    )
+    return jnp.sum(lax.all_to_all(copies, "z", 0, 0, tiled=True), axis=0)
 
 
 def solution(mesh):
-    in_specs = (P("vir", ("occ", "rep"), None), P("vir", None, ("occ", "rep")), P())
-    out_specs = P("occ", "rep")
+    grid = Mesh(mesh.devices.reshape(4, 8, 4, 2), ("x", "z", "occ", "rep"))
+    vir, group = ("x", "z"), ("occ", "rep")
     return jax.shard_map(
-        on_device, mesh=mesh, in_specs=in_specs, out_specs=out_specs, check_vma=False
+        on_device,
+        mesh=grid,
+        in_specs=(P(vir, group, None), P(vir, None, group), P()),
+        out_specs=P("occ", "rep"),
+        check_vma=False,
     )

time: 129 us -> 129 us (level); the launches traced: 128 us -> 127 us
  waiting for transfers between devices: 33.9 us -> 31.2 us
  starting transfers between devices: 16.9 us -> 19.4 us
  blocking collectives: 66.6 us -> 65.3 us
    ppermute x3, starting transfers between devices: 2.35 us -> 4.89 us  [on_device(): lax.ppermute(total, 'x', x_shift(k))]
    ppermute x3, waiting for transfers between devices: 4.48 us -> 2.28 us  [on_device(): lax.ppermute(total, 'x', x_shift(k))]
    all_to_all x2, blocking collectives: 58.1 us -> 56.2 us  [the longest x1 44.8 us: on_device(): lax.all_to_all(routed.reshape(VIR, SLOTS * GRP, LANE), ('z', 'x'), 0, 0,...]
where the time goes in v4:
time: 129 us; the launch traced here: 127 us
  blocking collectives  65.3 us (51%)
  waiting for transfers between devices  31.2 us (24%)
  starting transfers between devices  19.4 us (15%)
  Pallas kernels  8.81 us (7%)
    all_to_all x1, blocking collectives, on_device(): lax.all_to_all(routed.reshape(VIR, SLOTS * GRP, LANE), ('z', 'x'), 0, 0,...  44.8 us
    all_to_all x1, waiting for transfers between devices, on_device(): got = lax.all_to_all(sent, ('occ', 'rep', 'z', 'x'), 0, 0, tiled=True)  28.9 us
    all_to_all x1, starting transfers between devices, on_device(): got = lax.all_to_all(sent, ('occ', 'rep', 'z', 'x'), 0, 0, tiled=True)  14.6 us
    all_to_all x1, blocking collectives, on_device(): return jnp.sum(lax.all_to_all(copies, 'z', 0, 0, tiled=True), axis=0)  11.5 us
    all_to_all x1, blocking collectives, on_device(): lax.all_to_all(pieces, ('occ', 'rep'), 0, 0, tiled=True)  9.07 us
    pallas_call x1, Pallas kernels, contract(): pl.pallas_call(contract_kernel, out_shape=jax.ShapeDtypeStruct((GRP, 16,...  5.88 us
    ppermute x3, starting transfers between devices, on_device(): lax.ppermute(total, 'x', x_shift(k))  4.89 us
  transfers between devices with their start and end apart: 4, of which 4 were waited for; matrix products, arithmetic and copies ran while one was open for 0% of the time, Pallas kernels for 0%

profile of v4, /device:TPU:0, one launch (start us, length us, event | category | flops | bytes accessed | tf_op | source)
XLA Modules:
  0.0 126.9 jit_solution(17378309802246627211)
XLA Ops:
  0.0 0.0 copy-start
  0.0 1.2 copy-done
  1.2 1.6 %spread.1 = f32[2048,128]{1,0:T(8,128)} custom-call(f32[64,4096]{1,0:T(8,128)S(1)} %bitcast.9), custom_call_target="tpu_custom_call" | custom-call | bytes 2097152 | tf_op jit(solution)/shard_map/spread/pallas_call | solution.py:37
  2.8 0.0 copy-start.1
  2.8 14.6 %all-to-all-start = ((f32[256,8,128]{2,1,0:T(8,128)}), f32[256,8,128]{2,1,0:T(8,128)S(1)}, u32[]{:S(2)}, u32[]{:S(2)}) async-start(f32[256,8,128]{2,1,0:T(8,128)} %bitcast.2), calls=%async_computation | async-start | bytes 2097152 | tf_op jit(solution)/shard_map/all_to_all | solution.py:172
  17.4 0.0 copy-done.1
  17.4 0.2 select_reduce_fusion
  17.6 28.9 %all-to-all-done = f32[256,8,128]{2,1,0:T(8,128)S(1)} async-done(((f32[256,8,128]{2,1,0:T(8,128)}), f32[256,8,128]{2,1,0:T(8,128)S(1)}, u32[]{:S(2)}, u32[]{:S(2)}) %all-to-all-start) | async-done | bytes 1048608 | tf_op jit(solution)/shard_map/all_to_all | solution.py:172
  46.5 1.3 %route.1 = f32[384,8,128]{2,1,0:T(8,128)S(1)} custom-call(s32[256]{0:T(256)S(1)} %multiply_add_fusion.slot_ref, f32[2048,128]{1,0:T(8,128)S(1)} %bitcast.8), custom_call_target="tpu_custom_call" | custom-call | bytes 3145728 | tf_op jit(solution)/shard_map/route/pallas_call | solution.py:64
  47.8 44.8 %all_to_all.20 = f32[32,96,128]{2,1,0:T(8,128)S(1)} all-to-all(f32[32,96,128]{2,1,0:T(8,128)S(1)} %bitcast.6), channel_id=1, replica_groups=mesh['x'=4,'z'=8,'occ'=4,'rep'=2] {'z','x'}, dimensions={0} | all-to-all | bytes 3145728 | tf_op jit(solution)/shard_map/all_to_all | solution.py:174
  92.6 5.9 %contract.1 = f32[8,16,256]{2,1,0:T(8,128)S(1)} custom-call(f32[8,4,12,8,128]{4,3,2,1,0:T(8,128)S(1)} %bitcast.7, f32[12,512,512]{2,1,0:T(8,128)} %int_hbm.1), custom_call_target="tpu_custom_call" | custom-call | flops 1207959552 | bytes 14680064 | tf_op jit(solution)/shard_map/contract/pallas_call | solution.py:120
  98.5 9.1 %all_to_all.21 = f32[8,16,256]{2,1,0:T(8,128)S(1)} all-to-all(f32[8,16,256]{2,1,0:T(8,128)S(1)} %contract.1), channel_id=1, replica_groups=mesh['x'=4,'z'=8,'occ'=4,'rep'=2] {'occ','rep'}, dimensions={0} | all-to-all | bytes 262144 | tf_op jit(solution)/shard_map/all_to_all | solution.py:176
  107.6 0.7 collective-permute-start
  108.3 2.7 %collective-permute-start.1 = (f32[16,256]{1,0:T(8,128)S(1)}, f32[16,256]{1,0:T(8,128)S(1)}, u32[]{:S(2)}, u32[]{:S(2)}) collective-permute-start(f32[16,256]{1,0:T(8,128)S(1)} %reduce_sum.28.refs_0_), channel_id=1, source_target_pairs={{0,128},{64,192},{128,0},{192,64},{1,129},{65,193},{129,1},{193,65... | collective-permute-start | bytes 49160 | tf_op jit(solution)/shard_map/ppermute | solution.py:178
  111.0 1.5 %collective-permute-start.2 = (f32[16,256]{1,0:T(8,128)S(1)}, f32[16,256]{1,0:T(8,128)S(1)}, u32[]{:S(2)}, u32[]{:S(2)}) collective-permute-start(f32[16,256]{1,0:T(8,128)S(1)} %reduce_sum.28.refs_0_), channel_id=1, source_target_pairs={{0,192},{64,0},{128,64},{192,128},{1,193},{65,1},{129,65},{193,129... | collective-permute-start | bytes 49160 | tf_op jit(solution)/shard_map/ppermute | solution.py:178
  112.5 0.1 collective-permute-done.refs_1_
  112.6 1.0 collective-permute-done.1.refs_2_
  113.6 1.2 collective-permute-done.2.refs_3_
  114.8 11.5 %all_to_all.22 = f32[8,16,256]{2,1,0:T(8,128)S(1)} all-to-all(f32[8,16,256]{2,1,0:T(8,128)S(1)} %broadcast_in_dim.24), channel_id=1, replica_groups=mesh['x'=4,'z'=8,'occ'=4,'rep'=2] {'z'}, dimensions={0} | all-to-all | bytes 262144 | tf_op jit(solution)/shard_map/all_to_all | solution.py:181
  126.2 0.6 reduce_sum.29
  (4 shorter events, 0.1 us)
Async XLA Ops:
  0.0 1.2 copy-start
  2.8 14.6 %copy-start.1 = (s32[256]{0:T(256)S(1)}, s32[256]{0:T(256)}, u32[]{:S(2)}) copy-start(s32[256]{0:T(256)} %param.5) | copy-start | bytes 3076
  2.8 43.7 %all-to-all-start = ((f32[256,8,128]{2,1,0:T(8,128)}), f32[256,8,128]{2,1,0:T(8,128)S(1)}, u32[]{:S(2)}, u32[]{:S(2)}) async-start(f32[256,8,128]{2,1,0:T(8,128)} %bitcast.2), calls=%async_computation | async-start | bytes 2097152 | tf_op jit(solution)/shard_map/all_to_all | solution.py:172
  107.6 5.0 %collective-permute-start = (f32[16,256]{1,0:T(8,128)S(1)}, f32[16,256]{1,0:T(8,128)S(1)}, u32[]{:S(2)}, u32[]{:S(2)}) collective-permute-start(f32[16,256]{1,0:T(8,128)S(1)} %reduce_sum.28.refs_0_), channel_id=1, source_target_pairs={{0,64},{64,128},{128,192},{192,0},{1,65},{65,129},{129,193},{193,1... | collective-permute-start | bytes 49160 | tf_op jit(solution)/shard_map/ppermute | solution.py:178
  108.3 5.2 %collective-permute-start.1 = (f32[16,256]{1,0:T(8,128)S(1)}, f32[16,256]{1,0:T(8,128)S(1)}, u32[]{:S(2)}, u32[]{:S(2)}) collective-permute-start(f32[16,256]{1,0:T(8,128)S(1)} %reduce_sum.28.refs_0_), channel_id=1, source_target_pairs={{0,128},{64,192},{128,0},{192,64},{1,129},{65,193},{129,1},{193,65... | collective-permute-start | bytes 49160 | tf_op jit(solution)/shard_map/ppermute | solution.py:178
  111.0 3.7 %collective-permute-start.2 = (f32[16,256]{1,0:T(8,128)S(1)}, f32[16,256]{1,0:T(8,128)S(1)}, u32[]{:S(2)}, u32[]{:S(2)}) collective-permute-start(f32[16,256]{1,0:T(8,128)S(1)} %reduce_sum.28.refs_0_), channel_id=1, source_target_pairs={{0,192},{64,0},{128,64},{192,128},{1,193},{65,1},{129,65},{193,129... | collective-permute-start | bytes 49160 | tf_op jit(solution)/shard_map/ppermute | solution.py:178

commit v5 on v4

--- a/solution.py
+++ b/solution.py
@@ -23,23 +23,47 @@
     return (owners % 8 * 4 + owners // 8) * SLOTS + rank
 
 
-def spread_kernel(amp_ref, out_ref):
-    for blk in range(BLKS):
-        for chunk in range(32):
-            part, quarter = chunk // 4, chunk % 4
-            first = (part * VIR + quarter) * BLKS + blk
-            out_ref[pl.ds(first, 8, stride=4 * BLKS), :] = amp_ref[
-                pl.ds(blk * 8, 8), pl.ds(chunk * LANE, LANE)
-            ]
+def spread_kernel(amp_hbm, out_hbm, amp, out, in_sems, out_sems):
+    wide, rows = 4 * LANE, VIR * BLKS
+    arrive = [
+        pltpu.make_async_copy(
+            amp_hbm.at[:, pl.ds(part * wide, wide)], amp.at[part], in_sems.at[part]
+        )
+        for part in range(GRP)
+    ]
+    leave = [
+        pltpu.make_async_copy(
+            out.at[part], out_hbm.at[pl.ds(part * rows, rows)], out_sems.at[part]
+        )
+        for part in range(GRP)
+    ]
+    for copy in arrive:
+        copy.start()
+    for part in range(GRP):
+        arrive[part].wait()
+        for blk in range(BLKS):
+            for quarter in range(4):
+                out[part, pl.ds(quarter * BLKS + blk, 8, stride=4 * BLKS), :] = amp[
+                    part, pl.ds(blk * 8, 8), pl.ds(quarter * LANE, LANE)
+                ]
+        leave[part].start()
+    for copy in leave:
+        copy.wait()
 
 
 def spread(amp):
     return pl.pallas_call(
         spread_kernel,
         out_shape=jax.ShapeDtypeStruct((VIR * GRP * BLKS, LANE), jnp.float32),
-        in_specs=[pl.BlockSpec(memory_space=pltpu.VMEM)],
-        out_specs=pl.BlockSpec(memory_space=pltpu.VMEM),
-        compiler_params=pltpu.CompilerParams(vmem_limit_bytes=8 * MIB),
+        in_specs=[pl.BlockSpec(memory_space=pltpu.HBM)],
+        out_specs=pl.BlockSpec(memory_space=pltpu.HBM),
+        scratch_shapes=[
+            pltpu.VMEM((GRP, BLKS * 8, 4 * LANE), jnp.float32),
+            pltpu.VMEM((GRP, VIR * BLKS, LANE), jnp.float32),
+            pltpu.SemaphoreType.DMA((GRP,)),
+            pltpu.SemaphoreType.DMA((GRP,)),
+        ],
+        compiler_params=pltpu.CompilerParams(vmem_limit_bytes=60 * MIB),
         cost_estimate=pl.CostEstimate(flops=0, bytes_accessed=2 * MIB, transcendentals=0),
         name="spread",
     )(amp)
@@ -86,7 +110,7 @@
     )
 
 
-def contract_kernel(amp_ref, int_hbm, out_ref, held, acc, tiles, ordered, sems):
+def contract_kernel(amp_ref, int_hbm, out_ref, held, acc, tiles, sems):
     copies = [
         pltpu.make_async_copy(int_hbm.at[slot], held.at[slot], sems.at[slot])
         for slot in range(SLOTS)
@@ -107,19 +131,15 @@
         acc[...] += both[:64] + both[64:] + dot_nt(a_high, b_low)
     for tile in range(4):
         tiles[tile] = acc[:, pl.ds(tile * LANE, LANE)]
-    for tile in range(4):
-        for group in range(GRP):
-            ordered[tile // 2, pl.ds(group * 8, 8), pl.ds(tile % 2 * LANE, LANE)] = tiles[
-                tile, pl.ds(group, 8, stride=GRP), :
-            ]
-    for part in range(GRP):
-        out_ref[part] = ordered[part % 2, pl.ds(part // 2 * 16, 16), :]
+    for piece in range(VIR):
+        rep, occ, x = piece // 16, piece // 4 % 4, piece % 4
+        out_ref[piece] = tiles[rep * 2 + x % 2, pl.ds(occ * 2 + x // 2, 8, stride=GRP), :]
 
 
 def contract(amp, integrals):
     return pl.pallas_call(
         contract_kernel,
-        out_shape=jax.ShapeDtypeStruct((GRP, 16, 256), jnp.float32),
+        out_shape=jax.ShapeDtypeStruct((VIR, 8, LANE), jnp.float32),
         in_specs=[
             pl.BlockSpec(memory_space=pltpu.VMEM),
             pl.BlockSpec(memory_space=pltpu.HBM),
@@ -129,7 +149,6 @@
             pltpu.VMEM((SLOTS, 512, 512), jnp.float32),
             pltpu.VMEM((64, 512), jnp.float32),
             pltpu.VMEM((4, 64, LANE), jnp.float32),
-            pltpu.VMEM((2, 64, 256), jnp.float32),
             pltpu.SemaphoreType.DMA((SLOTS,)),
         ],
         compiler_params=pltpu.CompilerParams(vmem_limit_bytes=50 * MIB),
@@ -140,32 +159,34 @@
     )(amp, integrals)
 
 
-def sum_x_kernel(place_ref, *refs):
-    ins, out_ref, held = refs[:4], refs[4], refs[5]
-    for k in range(4):
-        held[lax.rem(place_ref[0] + 4 - k, 4)] = ins[k][...]
-    out_ref[...] = (held[0] + held[1]) + (held[2] + held[3])
-
-
-def sum_x(place, pieces):
-    return pl.pallas_call(
-        sum_x_kernel,
-        out_shape=jax.ShapeDtypeStruct((16, 256), jnp.float32),
-        in_specs=[pl.BlockSpec(memory_space=pltpu.SMEM)]
-        + [pl.BlockSpec(memory_space=pltpu.VMEM)] * 4,
+def add_up_kernel(got_ref, out_ref):
+    total = got_ref[0]
+    for i in range(1, VIR):
+        total = total + got_ref[i]
+    for i in range(VIR):
+        out_ref[i] = total
+
+
+def finish_kernel(got_ref, out_ref):
+    for x in range(4):
+        total = got_ref[x]
+        for z in range(1, 8):
+            total = total + got_ref[z * 4 + x]
+        out_ref[pl.ds(x // 2 * 8, 8), pl.ds(x % 2 * LANE, LANE)] = total
+
+
+def small(kernel, got, shape):
+    return pl.pallas_call(
+        kernel,
+        out_shape=jax.ShapeDtypeStruct(shape, jnp.float32),
+        in_specs=[pl.BlockSpec(memory_space=pltpu.VMEM)],
         out_specs=pl.BlockSpec(memory_space=pltpu.VMEM),
-        scratch_shapes=[pltpu.VMEM((4, 16, 256), jnp.float32)],
         compiler_params=pltpu.CompilerParams(vmem_limit_bytes=4 * MIB),
-        name="sum_x",
-    )(place, *pieces)
-
-
-def x_shift(k):
-    return [(x, (x + k) % 4) for x in range(4)]
+        name=kernel.__name__,
+    )(got)
 
 
 def on_device(amplitudes, integrals, block_owner):
-    x_place = lax.axis_index("x")[None]
     slot = slot_of_block(block_owner)
     sent = spread(amplitudes.reshape(BLKS * 8, 4096))
     sent = sent.reshape(VIR * GRP, BLKS, LANE)
@@ -173,12 +194,10 @@
     routed = route(slot, got.reshape(VIR * GRP * BLKS, LANE))
     owned = lax.all_to_all(routed.reshape(VIR, SLOTS * GRP, LANE), ("z", "x"), 0, 0, tiled=True)
     pieces = contract(owned.reshape(8, 4, SLOTS, GRP, LANE), integrals)
-    total = jnp.sum(lax.all_to_all(pieces, ("occ", "rep"), 0, 0, tiled=True), axis=0)
-    total = sum_x(
-        x_place, [total] + [lax.ppermute(total, "x", x_shift(k)) for k in range(1, 4)]
-    )
-    copies = jnp.broadcast_to(total[None], (8, 16, 256))
-    return jnp.sum(lax.all_to_all(copies, "z", 0, 0, tiled=True), axis=0)
+    parts = lax.all_to_all(pieces, ("rep", "occ", "x"), 0, 0, tiled=True)
+    copies = small(add_up_kernel, parts, (VIR, 8, LANE))
+    parts = lax.all_to_all(copies, ("z", "x"), 0, 0, tiled=True)
+    return small(finish_kernel, parts, (16, 256))
 
 
 def solution(mesh):

time: 129 us -> 127 us (0.984)
  blocking collectives: 65.3 us -> 71.6 us
  starting transfers between devices: 19.4 us -> 14.6 us
  waiting for transfers between devices: 31.2 us -> 28.9 us
  Pallas kernels: 8.81 us -> 10.2 us
    all_to_all x2, blocking collectives: 20.5 us -> 26.9 us  [the longest x1 14.1 us: on_device(): parts = lax.all_to_all(copies, ('z', 'x'), 0, 0, tiled=True)]
    ppermute x3 -> x0, starting transfers between devices: 4.89 us -> none  [on_device(): lax.ppermute(total, 'x', x_shift(k))]
    ppermute x3 -> x0, waiting for transfers between devices: 2.28 us -> none  [on_device(): lax.ppermute(total, 'x', x_shift(k))]
    pallas_call x2 -> x3, Pallas kernels: 5.89 us -> 6.54 us  [the longest x1 5.88 us: contract(): pl.pallas_call(contract_kernel, out_shape=jax.ShapeDtypeStruct((VIR, 8, L...]
  transfers between devices with their start and end apart: 4 -> 1, of which waited for: 4 -> 1; matrix products, arithmetic and copies ran while one was open for 0% -> 0% of each run, Pallas kernels for 0% -> 0%
where the time goes in v5:
time: 127 us; the launch traced here: 126 us
  blocking collectives  71.6 us (56%)
  waiting for transfers between devices  28.9 us (23%)
  starting transfers between devices  14.6 us (11%)
  Pallas kernels  10.2 us (8%)
    all_to_all x1, blocking collectives, on_device(): lax.all_to_all(routed.reshape(VIR, SLOTS * GRP, LANE), ('z', 'x'), 0, 0,...  44.8 us
    all_to_all x1, waiting for transfers between devices, on_device(): got = lax.all_to_all(sent, ('occ', 'rep', 'z', 'x'), 0, 0, tiled=True)  28.9 us
    all_to_all x1, starting transfers between devices, on_device(): got = lax.all_to_all(sent, ('occ', 'rep', 'z', 'x'), 0, 0, tiled=True)  14.6 us
    all_to_all x1, blocking collectives, on_device(): parts = lax.all_to_all(copies, ('z', 'x'), 0, 0, tiled=True)  14.1 us
    all_to_all x1, blocking collectives, on_device(): parts = lax.all_to_all(pieces, ('rep', 'occ', 'x'), 0, 0, tiled=True)  12.8 us
    pallas_call x1, Pallas kernels, contract(): pl.pallas_call(contract_kernel, out_shape=jax.ShapeDtypeStruct((VIR, 8, L...  5.88 us
  transfers between devices with their start and end apart: 1, of which 1 were waited for; matrix products, arithmetic and copies ran while one was open for 0% of the time, Pallas kernels for 0%

profile of v5, /device:TPU:0, one launch (start us, length us, event | category | flops | bytes accessed | tf_op | source)
XLA Modules:
  0.0 125.6 jit_solution(5705287245367073177)
XLA Ops:
  0.0 2.4 %spread.1 = f32[2048,128]{1,0:T(8,128)} custom-call(f32[64,4096]{1,0:T(8,128)} %bitcast.9), custom_call_target="tpu_custom_call" | custom-call | bytes 2097152 | tf_op jit(solution)/shard_map/spread/pallas_call | solution.py:55
  2.4 0.0 copy-start
  2.4 14.6 %all-to-all-start = ((f32[256,8,128]{2,1,0:T(8,128)}), f32[256,8,128]{2,1,0:T(8,128)S(1)}, u32[]{:S(2)}, u32[]{:S(2)}) async-start(f32[256,8,128]{2,1,0:T(8,128)} %bitcast.8), calls=%async_computation | async-start | bytes 2097152 | tf_op jit(solution)/shard_map/all_to_all | solution.py:193
  16.9 0.0 copy-done
  17.0 0.2 select_reduce_fusion
  17.2 28.9 %all-to-all-done = f32[256,8,128]{2,1,0:T(8,128)S(1)} async-done(((f32[256,8,128]{2,1,0:T(8,128)}), f32[256,8,128]{2,1,0:T(8,128)S(1)}, u32[]{:S(2)}, u32[]{:S(2)}) %all-to-all-start) | async-done | bytes 1048608 | tf_op jit(solution)/shard_map/all_to_all | solution.py:193
  46.1 1.3 %route.1 = f32[384,8,128]{2,1,0:T(8,128)S(1)} custom-call(s32[256]{0:T(256)S(1)} %multiply_add_fusion.slot_ref, f32[2048,128]{1,0:T(8,128)S(1)} %bitcast.7), custom_call_target="tpu_custom_call" | custom-call | bytes 3145728 | tf_op jit(solution)/shard_map/route/pallas_call | solution.py:88
  47.4 44.8 %all_to_all.20 = f32[32,96,128]{2,1,0:T(8,128)S(1)} all-to-all(f32[32,96,128]{2,1,0:T(8,128)S(1)} %bitcast.5), channel_id=1, replica_groups=mesh['x'=4,'z'=8,'occ'=4,'rep'=2] {'z','x'}, dimensions={0} | all-to-all | bytes 3145728 | tf_op jit(solution)/shard_map/all_to_all | solution.py:195
  92.2 5.9 %contract.1 = f32[32,8,128]{2,1,0:T(8,128)S(1)} custom-call(f32[8,4,12,8,128]{4,3,2,1,0:T(8,128)S(1)} %bitcast.6, f32[12,512,512]{2,1,0:T(8,128)} %int_hbm.1), custom_call_target="tpu_custom_call" | custom-call | flops 1207959552 | bytes 14680064 | tf_op jit(solution)/shard_map/contract/pallas_call | solution.py:140
  98.1 12.8 %all_to_all.21.got_ref = f32[32,8,128]{2,1,0:T(8,128)S(1)} all-to-all(f32[32,8,128]{2,1,0:T(8,128)S(1)} %contract.1), channel_id=1, replica_groups=mesh['x'=4,'z'=8,'occ'=4,'rep'=2] {'rep','occ','x'}, dimensions={0} | all-to-all | bytes 262144 | tf_op jit(solution)/shard_map/all_to_all | solution.py:197
  110.9 14.1 %all_to_all.22.got_ref = f32[32,8,128]{2,1,0:T(8,128)S(1)} all-to-all(f32[32,8,128]{2,1,0:T(8,128)S(1)} %add_up_kernel.1), channel_id=1, replica_groups=mesh['x'=4,'z'=8,'occ'=4,'rep'=2] {'z','x'}, dimensions={0} | all-to-all | bytes 262144 | tf_op jit(solution)/shard_map/all_to_all | solution.py:199
  125.0 0.6 finish_kernel.1
  (2 shorter events, 0.1 us)
Async XLA Ops:
  2.4 14.6 %copy-start = (s32[256]{0:T(256)S(1)}, s32[256]{0:T(256)}, u32[]{:S(2)}) copy-start(s32[256]{0:T(256)} %param.5) | copy-start | bytes 3076
  2.4 43.7 %all-to-all-start = ((f32[256,8,128]{2,1,0:T(8,128)}), f32[256,8,128]{2,1,0:T(8,128)S(1)}, u32[]{:S(2)}, u32[]{:S(2)}) async-start(f32[256,8,128]{2,1,0:T(8,128)} %bitcast.8), calls=%async_computation | async-start | bytes 2097152 | tf_op jit(solution)/shard_map/all_to_all | solution.py:193

commit v6 on v5

--- a/solution.py
+++ b/solution.py
@@ -11,62 +11,63 @@
 BLKS = 8
 SLOTS = 12
 LANE = 128
-AHEAD = 6
+AHEAD = 12
 MIB = 1 << 20
 
 
-def slot_of_block(owners):
-    ids = jnp.arange(owners.shape[0], dtype=jnp.int32)
-    earlier = ids[None, :] < ids[:, None]
-    same = owners[None, :] == owners[:, None]
-    rank = jnp.sum(jnp.where(same & earlier, 1, 0), axis=1).astype(jnp.int32)
-    return (owners % 8 * 4 + owners // 8) * SLOTS + rank
-
-
-def spread_kernel(amp_hbm, out_hbm, amp, out, in_sems, out_sems):
-    wide, rows = 4 * LANE, VIR * BLKS
-    arrive = [
+def spread_kernel(owner_hbm, amp_hbm, slot_ref, out_ref, owner_ref, amp, sems):
+    wide = 4 * LANE
+    copies = [
         pltpu.make_async_copy(
-            amp_hbm.at[:, pl.ds(part * wide, wide)], amp.at[part], in_sems.at[part]
+            amp_hbm.at[:, pl.ds(part * wide, wide)], amp.at[part], sems.at[part]
         )
         for part in range(GRP)
     ]
-    leave = [
-        pltpu.make_async_copy(
-            out.at[part], out_hbm.at[pl.ds(part * rows, rows)], out_sems.at[part]
-        )
-        for part in range(GRP)
-    ]
-    for copy in arrive:
+    owner_copy = pltpu.make_async_copy(owner_hbm, owner_ref, sems.at[GRP])
+    owner_copy.start()
+    for copy in copies:
         copy.start()
+
+    owner_copy.wait()
+    count = owner_ref.shape[1]
+    owners = owner_ref[...]
+    along = jnp.broadcast_to(owners.astype(jnp.float32), (count, count))
+    down = along.T
+    rows = lax.broadcasted_iota(jnp.int32, (count, count), 0)
+    lanes = lax.broadcasted_iota(jnp.int32, (count, count), 1)
+    earlier = jnp.where((down == along) & (rows < lanes), 1, 0)
+    rank = jnp.sum(earlier, axis=0, keepdims=True)
+    place = lax.rem(owners, 8) * 4 + lax.div(owners, 8)
+    slot_ref[...] = place * SLOTS + rank
+
     for part in range(GRP):
-        arrive[part].wait()
+        copies[part].wait()
         for blk in range(BLKS):
             for quarter in range(4):
-                out[part, pl.ds(quarter * BLKS + blk, 8, stride=4 * BLKS), :] = amp[
+                first = (part * VIR + quarter) * BLKS + blk
+                out_ref[pl.ds(first, 8, stride=4 * BLKS), :] = amp[
                     part, pl.ds(blk * 8, 8), pl.ds(quarter * LANE, LANE)
                 ]
-        leave[part].start()
-    for copy in leave:
-        copy.wait()
-
-
-def spread(amp):
+
+
+def spread(owners, amp):
     return pl.pallas_call(
         spread_kernel,
-        out_shape=jax.ShapeDtypeStruct((VIR * GRP * BLKS, LANE), jnp.float32),
-        in_specs=[pl.BlockSpec(memory_space=pltpu.HBM)],
-        out_specs=pl.BlockSpec(memory_space=pltpu.HBM),
+        out_shape=[
+            jax.ShapeDtypeStruct(owners.shape, jnp.int32),
+            jax.ShapeDtypeStruct((VIR * GRP * BLKS, LANE), jnp.float32),
+        ],
+        in_specs=[pl.BlockSpec(memory_space=pltpu.HBM)] * 2,
+        out_specs=[pl.BlockSpec(memory_space=pltpu.VMEM)] * 2,
         scratch_shapes=[
+            pltpu.VMEM(owners.shape, jnp.int32),
             pltpu.VMEM((GRP, BLKS * 8, 4 * LANE), jnp.float32),
-            pltpu.VMEM((GRP, VIR * BLKS, LANE), jnp.float32),
-            pltpu.SemaphoreType.DMA((GRP,)),
-            pltpu.SemaphoreType.DMA((GRP,)),
-        ],
-        compiler_params=pltpu.CompilerParams(vmem_limit_bytes=60 * MIB),
+            pltpu.SemaphoreType.DMA((GRP + 1,)),
+        ],
+        compiler_params=pltpu.CompilerParams(vmem_limit_bytes=52 * MIB),
         cost_estimate=pl.CostEstimate(flops=0, bytes_accessed=2 * MIB, transcendentals=0),
         name="spread",
-    )(amp)
+    )(owners, amp)
 
 
 def route_kernel(slot_ref, got_ref, out_ref):
@@ -79,7 +80,7 @@
     for source in range(VIR):
         for blk in range(BLKS):
             vir = source % 4 * 8 + source // 4
-            out_ref[slot_ref[vir * BLKS + blk]] = got_ref[
+            out_ref[slot_ref[0, vir * BLKS + blk]] = got_ref[
                 pl.ds(source * BLKS + blk, GRP, stride=VIR * BLKS), :
             ]
 
@@ -110,7 +111,7 @@
     )
 
 
-def contract_kernel(amp_ref, int_hbm, out_ref, held, acc, tiles, sems):
+def contract_kernel(amp_ref, int_hbm, out_ref, held, pair, acc, tiles, sems):
     copies = [
         pltpu.make_async_copy(int_hbm.at[slot], held.at[slot], sems.at[slot])
         for slot in range(SLOTS)
@@ -122,13 +123,14 @@
         rows = jnp.concatenate(
             [amp_ref[:, q, slot].reshape(64, LANE) for q in range(4)], axis=1
         )
-        a_high, a_low = split(rows)
+        pair[slot] = jnp.concatenate(split(rows), axis=0)
+    for slot in range(SLOTS):
         copies[slot].wait()
         if slot + AHEAD < SLOTS:
             copies[slot + AHEAD].start()
         b_high, b_low = split(held[slot])
-        both = dot_nt(jnp.concatenate([a_high, a_low], axis=0), b_high)
-        acc[...] += both[:64] + both[64:] + dot_nt(a_high, b_low)
+        both = dot_nt(pair[slot], b_high)
+        acc[...] += both[:64] + both[64:] + dot_nt(pair[slot, :64], b_low)
     for tile in range(4):
         tiles[tile] = acc[:, pl.ds(tile * LANE, LANE)]
     for piece in range(VIR):
@@ -147,6 +149,7 @@
         out_specs=pl.BlockSpec(memory_space=pltpu.VMEM),
         scratch_shapes=[
             pltpu.VMEM((SLOTS, 512, 512), jnp.float32),
+            pltpu.VMEM((SLOTS, 128, 512), jnp.bfloat16),
             pltpu.VMEM((64, 512), jnp.float32),
             pltpu.VMEM((4, 64, LANE), jnp.float32),
             pltpu.SemaphoreType.DMA((SLOTS,)),
@@ -187,8 +190,7 @@
 
 
 def on_device(amplitudes, integrals, block_owner):
-    slot = slot_of_block(block_owner)
-    sent = spread(amplitudes.reshape(BLKS * 8, 4096))
+    slot, sent = spread(block_owner.reshape(1, -1), amplitudes.reshape(BLKS * 8, 4096))
     sent = sent.reshape(VIR * GRP, BLKS, LANE)
     got = lax.all_to_all(sent, ("occ", "rep", "z", "x"), 0, 0, tiled=True)
     routed = route(slot, got.reshape(VIR * GRP * BLKS, LANE))

time: 127 us -> 127 us (level)
  blocking collectives: 71.6 us -> 115 us
  waiting for transfers between devices: 28.9 us -> 0 us
  starting transfers between devices: 14.6 us -> 0 us
    all_to_all x0 -> x1, blocking collectives: none -> 43.5 us  [on_device(): got = lax.all_to_all(sent, ('occ', 'rep', 'z', 'x'), 0, 0, tiled=True)]
    all_to_all x1 -> x0, waiting for transfers between devices: 28.9 us -> none  [on_device(): got = lax.all_to_all(sent, ('occ', 'rep', 'z', 'x'), 0, 0, tiled=True)]
    all_to_all x1 -> x0, starting transfers between devices: 14.6 us -> none  [on_device(): got = lax.all_to_all(sent, ('occ', 'rep', 'z', 'x'), 0, 0, tiled=True)]
  transfers between devices with their start and end apart: 1 -> 0, of which waited for: 1 -> 0; matrix products, arithmetic and copies ran while one was open for 0% -> 0% of each run, Pallas kernels for 0% -> 0%
where the time goes in v6:
time: 127 us; the launch traced here: 125 us
  blocking collectives  115 us (91%)
  Pallas kernels  9.27 us (7%)
    all_to_all x1, blocking collectives, on_device(): lax.all_to_all(routed.reshape(VIR, SLOTS * GRP, LANE), ('z', 'x'), 0, 0,...  44.8 us
    all_to_all x1, blocking collectives, on_device(): got = lax.all_to_all(sent, ('occ', 'rep', 'z', 'x'), 0, 0, tiled=True)  43.5 us
    all_to_all x1, blocking collectives, on_device(): parts = lax.all_to_all(copies, ('z', 'x'), 0, 0, tiled=True)  14.1 us
    all_to_all x1, blocking collectives, on_device(): parts = lax.all_to_all(pieces, ('rep', 'occ', 'x'), 0, 0, tiled=True)  12.8 us
    pallas_call x1, Pallas kernels, contract(): pl.pallas_call(contract_kernel, out_shape=jax.ShapeDtypeStruct((VIR, 8, L...  5.65 us

profile of v6, /device:TPU:0, one launch (start us, length us, event | category | flops | bytes accessed | tf_op | source)
XLA Modules:
  0.0 125.1 jit_solution(18295888576681065341)
XLA Ops:
  0.0 0.0 copy-start
  0.0 0.7 copy-done
  0.7 1.6 %spread.1 = (s32[1,256]{1,0:T(1,128)S(1)}, f32[2048,128]{1,0:T(8,128)S(1)}) custom-call(s32[1,256]{1,0:T(1,128)S(1)} %bitcast.10, f32[64,4096]{1,0:T(8,128)} %bitcast.11), custom_call_target="tpu_custom_call" | custom-call | bytes 2097152 | tf_op jit(solution)/shard_map/spread/pallas_call | solution.py:54
  2.3 43.5 %all_to_all.20 = f32[256,8,128]{2,1,0:T(8,128)S(1)} all-to-all(f32[256,8,128]{2,1,0:T(8,128)S(1)} %bitcast.9), channel_id=1, replica_groups=mesh['x'=4,'z'=8,'occ'=4,'rep'=2] {'occ','rep','z','x'}, dimensions={0} | all-to-all | bytes 2097152 | tf_op jit(solution)/shard_map/all_to_all | solution.py:195
  45.8 1.3 %route.1 = f32[384,8,128]{2,1,0:T(8,128)S(1)} custom-call(s32[1,256]{1,0:T(1,128)S(1)} %get-tuple-element.7.slot_ref, f32[2048,128]{1,0:T(8,128)S(1)} %bitcast.8), custom_call_target="tpu_custom_call" | custom-call | bytes 3145728 | tf_op jit(solution)/shard_map/route/pallas_call | solution.py:89
  47.1 44.8 %all_to_all.21 = f32[32,96,128]{2,1,0:T(8,128)S(1)} all-to-all(f32[32,96,128]{2,1,0:T(8,128)S(1)} %bitcast.6), channel_id=1, replica_groups=mesh['x'=4,'z'=8,'occ'=4,'rep'=2] {'z','x'}, dimensions={0} | all-to-all | bytes 3145728 | tf_op jit(solution)/shard_map/all_to_all | solution.py:197
  91.9 5.6 %contract.1 = f32[32,8,128]{2,1,0:T(8,128)S(1)} custom-call(f32[8,4,12,8,128]{4,3,2,1,0:T(8,128)S(1)} %bitcast.7, f32[12,512,512]{2,1,0:T(8,128)} %int_hbm.1), custom_call_target="tpu_custom_call" | custom-call | flops 1207959552 | bytes 14680064 | tf_op jit(solution)/shard_map/contract/pallas_call | solution.py:142
  97.6 12.8 %all_to_all.22.got_ref = f32[32,8,128]{2,1,0:T(8,128)S(1)} all-to-all(f32[32,8,128]{2,1,0:T(8,128)S(1)} %contract.1), channel_id=1, replica_groups=mesh['x'=4,'z'=8,'occ'=4,'rep'=2] {'rep','occ','x'}, dimensions={0} | all-to-all | bytes 262144 | tf_op jit(solution)/shard_map/all_to_all | solution.py:199
  110.4 14.1 %all_to_all.23.got_ref = f32[32,8,128]{2,1,0:T(8,128)S(1)} all-to-all(f32[32,8,128]{2,1,0:T(8,128)S(1)} %add_up_kernel.1), channel_id=1, replica_groups=mesh['x'=4,'z'=8,'occ'=4,'rep'=2] {'z','x'}, dimensions={0} | all-to-all | bytes 262144 | tf_op jit(solution)/shard_map/all_to_all | solution.py:201
  124.5 0.6 finish_kernel.1
  (1 shorter events, 0.0 us)
Async XLA Ops:
  0.0 0.7 copy-start

commit v7 on v6

--- a/solution.py
+++ b/solution.py
@@ -44,8 +44,8 @@
         copies[part].wait()
         for blk in range(BLKS):
             for quarter in range(4):
-                first = (part * VIR + quarter) * BLKS + blk
-                out_ref[pl.ds(first, 8, stride=4 * BLKS), :] = amp[
+                first = (quarter * GRP + part) * 8 * BLKS + blk
+                out_ref[pl.ds(first, 8, stride=BLKS), :] = amp[
                     part, pl.ds(blk * 8, 8), pl.ds(quarter * LANE, LANE)
                 ]
 
@@ -79,9 +79,10 @@
 
     for source in range(VIR):
         for blk in range(BLKS):
-            vir = source % 4 * 8 + source // 4
+            x, z = source % 4, source // 4
+            vir = x * 8 + z
             out_ref[slot_ref[0, vir * BLKS + blk]] = got_ref[
-                pl.ds(source * BLKS + blk, GRP, stride=VIR * BLKS), :
+                pl.ds((x * GRP * 8 + z) * BLKS + blk, GRP, stride=8 * BLKS), :
             ]
 
 
@@ -192,7 +193,7 @@
 def on_device(amplitudes, integrals, block_owner):
     slot, sent = spread(block_owner.reshape(1, -1), amplitudes.reshape(BLKS * 8, 4096))
     sent = sent.reshape(VIR * GRP, BLKS, LANE)
-    got = lax.all_to_all(sent, ("occ", "rep", "z", "x"), 0, 0, tiled=True)
+    got = lax.all_to_all(sent, ("x", "occ", "rep", "z"), 0, 0, tiled=True)
     routed = route(slot, got.reshape(VIR * GRP * BLKS, LANE))
     owned = lax.all_to_all(routed.reshape(VIR, SLOTS * GRP, LANE), ("z", "x"), 0, 0, tiled=True)
     pieces = contract(owned.reshape(8, 4, SLOTS, GRP, LANE), integrals)

time: 127 us -> 127 us (level)
    all_to_all x1, blocking collectives: 43.5 us -> 45.3 us  [on_device(): got = lax.all_to_all(sent, ('x', 'occ', 'rep', 'z'), 0, 0, tiled=True)]
    all_to_all x1, blocking collectives: 44.8 us -> 43.3 us  [on_device(): lax.all_to_all(routed.reshape(VIR, SLOTS * GRP, LANE), ('z', 'x'), 0, 0,...]
where the time goes in v7:
time: 127 us; the launch traced here: 125 us
  blocking collectives  116 us (91%)
  Pallas kernels  9.03 us (7%)
    all_to_all x1, blocking collectives, on_device(): got = lax.all_to_all(sent, ('x', 'occ', 'rep', 'z'), 0, 0, tiled=True)  45.3 us
    all_to_all x1, blocking collectives, on_device(): lax.all_to_all(routed.reshape(VIR, SLOTS * GRP, LANE), ('z', 'x'), 0, 0,...  43.3 us
    all_to_all x1, blocking collectives, on_device(): parts = lax.all_to_all(copies, ('z', 'x'), 0, 0, tiled=True)  14.1 us
    all_to_all x1, blocking collectives, on_device(): parts = lax.all_to_all(pieces, ('rep', 'occ', 'x'), 0, 0, tiled=True)  12.9 us
    pallas_call x1, Pallas kernels, contract(): pl.pallas_call(contract_kernel, out_shape=jax.ShapeDtypeStruct((VIR, 8, L...  5.65 us

profile of v7, /device:TPU:0, one launch (start us, length us, event | category | flops | bytes accessed | tf_op | source)
XLA Modules:
  0.0 125.3 jit_solution(11424400998042592473)
XLA Ops:
  0.0 0.0 copy-start
  0.0 0.7 copy-done
  0.7 1.4 %spread.1 = (s32[1,256]{1,0:T(1,128)S(1)}, f32[2048,128]{1,0:T(8,128)S(1)}) custom-call(s32[1,256]{1,0:T(1,128)S(1)} %bitcast.10, f32[64,4096]{1,0:T(8,128)} %bitcast.11), custom_call_target="tpu_custom_call" | custom-call | bytes 2097152 | tf_op jit(solution)/shard_map/spread/pallas_call | solution.py:54
  2.1 45.3 %all_to_all.20 = f32[256,8,128]{2,1,0:T(8,128)S(1)} all-to-all(f32[256,8,128]{2,1,0:T(8,128)S(1)} %bitcast.9), channel_id=1, replica_groups=mesh['x'=4,'z'=8,'occ'=4,'rep'=2] {'x','occ','rep','z'}, dimensions={0} | all-to-all | bytes 2097152 | tf_op jit(solution)/shard_map/all_to_all | solution.py:196
  47.3 1.3 %route.1 = f32[384,8,128]{2,1,0:T(8,128)S(1)} custom-call(s32[1,256]{1,0:T(1,128)S(1)} %get-tuple-element.7.slot_ref, f32[2048,128]{1,0:T(8,128)S(1)} %bitcast.8), custom_call_target="tpu_custom_call" | custom-call | bytes 3145728 | tf_op jit(solution)/shard_map/route/pallas_call | solution.py:90
  48.7 43.3 %all_to_all.21 = f32[32,96,128]{2,1,0:T(8,128)S(1)} all-to-all(f32[32,96,128]{2,1,0:T(8,128)S(1)} %bitcast.6), channel_id=1, replica_groups=mesh['x'=4,'z'=8,'occ'=4,'rep'=2] {'z','x'}, dimensions={0} | all-to-all | bytes 3145728 | tf_op jit(solution)/shard_map/all_to_all | solution.py:198
  91.9 5.6 %contract.1 = f32[32,8,128]{2,1,0:T(8,128)S(1)} custom-call(f32[8,4,12,8,128]{4,3,2,1,0:T(8,128)S(1)} %bitcast.7, f32[12,512,512]{2,1,0:T(8,128)} %int_hbm.1), custom_call_target="tpu_custom_call" | custom-call | flops 1207959552 | bytes 14680064 | tf_op jit(solution)/shard_map/contract/pallas_call | solution.py:143
  97.6 12.9 %all_to_all.22.got_ref = f32[32,8,128]{2,1,0:T(8,128)S(1)} all-to-all(f32[32,8,128]{2,1,0:T(8,128)S(1)} %contract.1), channel_id=1, replica_groups=mesh['x'=4,'z'=8,'occ'=4,'rep'=2] {'rep','occ','x'}, dimensions={0} | all-to-all | bytes 262144 | tf_op jit(solution)/shard_map/all_to_all | solution.py:200
  110.5 14.1 %all_to_all.23.got_ref = f32[32,8,128]{2,1,0:T(8,128)S(1)} all-to-all(f32[32,8,128]{2,1,0:T(8,128)S(1)} %add_up_kernel.1), channel_id=1, replica_groups=mesh['x'=4,'z'=8,'occ'=4,'rep'=2] {'z','x'}, dimensions={0} | all-to-all | bytes 262144 | tf_op jit(solution)/shard_map/all_to_all | solution.py:202
  124.7 0.6 finish_kernel.1
  (1 shorter events, 0.0 us)
Async XLA Ops:
  0.0 0.7 copy-start

commit v8 on v7

--- a/solution.py
+++ b/solution.py
@@ -15,7 +15,7 @@
 MIB = 1 << 20
 
 
-def spread_kernel(owner_hbm, amp_hbm, slot_ref, out_ref, owner_ref, amp, sems):
+def spread_kernel(amp_hbm, out_ref, amp, sems):
     wide = 4 * LANE
     copies = [
         pltpu.make_async_copy(
@@ -23,12 +23,36 @@
         )
         for part in range(GRP)
     ]
-    owner_copy = pltpu.make_async_copy(owner_hbm, owner_ref, sems.at[GRP])
-    owner_copy.start()
     for copy in copies:
         copy.start()
 
-    owner_copy.wait()
+    for part in range(GRP):
+        copies[part].wait()
+        for blk in range(BLKS):
+            for quarter in range(4):
+                first = (quarter * GRP + part) * 8 * BLKS + blk
+                out_ref[pl.ds(first, 8, stride=BLKS), :] = amp[
+                    part, pl.ds(blk * 8, 8), pl.ds(quarter * LANE, LANE)
+                ]
+
+
+def spread(amp):
+    return pl.pallas_call(
+        spread_kernel,
+        out_shape=jax.ShapeDtypeStruct((VIR * GRP * BLKS, LANE), jnp.float32),
+        in_specs=[pl.BlockSpec(memory_space=pltpu.HBM)],
+        out_specs=pl.BlockSpec(memory_space=pltpu.VMEM),
+        scratch_shapes=[
+            pltpu.VMEM((GRP, BLKS * 8, 4 * LANE), jnp.float32),
+            pltpu.SemaphoreType.DMA((GRP,)),
+        ],
+        compiler_params=pltpu.CompilerParams(vmem_limit_bytes=52 * MIB),
+        cost_estimate=pl.CostEstimate(flops=0, bytes_accessed=2 * MIB, transcendentals=0),
+        name="spread",
+    )(amp)
+
+
+def route_kernel(owner_ref, got_ref, out_ref, slots, slot_ref, sem):
     count = owner_ref.shape[1]
     owners = owner_ref[...]
     along = jnp.broadcast_to(owners.astype(jnp.float32), (count, count))
@@ -38,44 +62,16 @@
     earlier = jnp.where((down == along) & (rows < lanes), 1, 0)
     rank = jnp.sum(earlier, axis=0, keepdims=True)
     place = lax.rem(owners, 8) * 4 + lax.div(owners, 8)
-    slot_ref[...] = place * SLOTS + rank
-
-    for part in range(GRP):
-        copies[part].wait()
-        for blk in range(BLKS):
-            for quarter in range(4):
-                first = (quarter * GRP + part) * 8 * BLKS + blk
-                out_ref[pl.ds(first, 8, stride=BLKS), :] = amp[
-                    part, pl.ds(blk * 8, 8), pl.ds(quarter * LANE, LANE)
-                ]
-
-
-def spread(owners, amp):
-    return pl.pallas_call(
-        spread_kernel,
-        out_shape=[
-            jax.ShapeDtypeStruct(owners.shape, jnp.int32),
-            jax.ShapeDtypeStruct((VIR * GRP * BLKS, LANE), jnp.float32),
-        ],
-        in_specs=[pl.BlockSpec(memory_space=pltpu.HBM)] * 2,
-        out_specs=[pl.BlockSpec(memory_space=pltpu.VMEM)] * 2,
-        scratch_shapes=[
-            pltpu.VMEM(owners.shape, jnp.int32),
-            pltpu.VMEM((GRP, BLKS * 8, 4 * LANE), jnp.float32),
-            pltpu.SemaphoreType.DMA((GRP + 1,)),
-        ],
-        compiler_params=pltpu.CompilerParams(vmem_limit_bytes=52 * MIB),
-        cost_estimate=pl.CostEstimate(flops=0, bytes_accessed=2 * MIB, transcendentals=0),
-        name="spread",
-    )(owners, amp)
-
-
-def route_kernel(slot_ref, got_ref, out_ref):
+    slots[...] = place * SLOTS + rank
+    to_scalars = pltpu.make_async_copy(slots, slot_ref, sem)
+    to_scalars.start()
+
     def clear(i, carry):
         out_ref[pl.ds(i * SLOTS, SLOTS)] = jnp.zeros((SLOTS, GRP, LANE), jnp.float32)
         return carry
 
     lax.fori_loop(0, VIR, clear, 0)
+    to_scalars.wait()
 
     for source in range(VIR):
         for blk in range(BLKS):
@@ -86,19 +82,24 @@
             ]
 
 
-def route(slot, got):
+def route(owners, got):
     return pl.pallas_call(
         route_kernel,
         out_shape=jax.ShapeDtypeStruct((VIR * SLOTS, GRP, LANE), jnp.float32),
         in_specs=[
-            pl.BlockSpec(memory_space=pltpu.SMEM),
             pl.BlockSpec(memory_space=pltpu.VMEM),
-        ],
-        out_specs=pl.BlockSpec(memory_space=pltpu.VMEM),
+            pl.BlockSpec(memory_space=pltpu.VMEM),
+        ],
+        out_specs=pl.BlockSpec(memory_space=pltpu.VMEM),
+        scratch_shapes=[
+            pltpu.VMEM(owners.shape, jnp.int32),
+            pltpu.SMEM(owners.shape, jnp.int32),
+            pltpu.SemaphoreType.DMA,
+        ],
         compiler_params=pltpu.CompilerParams(vmem_limit_bytes=8 * MIB),
         cost_estimate=pl.CostEstimate(flops=0, bytes_accessed=3 * MIB, transcendentals=0),
         name="route",
-    )(slot, got)
+    )(owners, got)
 
 
 def split(value):
@@ -191,10 +192,10 @@
 
 
 def on_device(amplitudes, integrals, block_owner):
-    slot, sent = spread(block_owner.reshape(1, -1), amplitudes.reshape(BLKS * 8, 4096))
+    sent = spread(amplitudes.reshape(BLKS * 8, 4096))
     sent = sent.reshape(VIR * GRP, BLKS, LANE)
     got = lax.all_to_all(sent, ("x", "occ", "rep", "z"), 0, 0, tiled=True)
-    routed = route(slot, got.reshape(VIR * GRP * BLKS, LANE))
+    routed = route(block_owner.reshape(1, -1), got.reshape(VIR * GRP * BLKS, LANE))
     owned = lax.all_to_all(routed.reshape(VIR, SLOTS * GRP, LANE), ("z", "x"), 0, 0, tiled=True)
     pieces = contract(owned.reshape(8, 4, SLOTS, GRP, LANE), integrals)
     parts = lax.all_to_all(pieces, ("rep", "occ", "x"), 0, 0, tiled=True)

time: 127 us -> 126 us (level)
  no operation moved by 1% of the time
where the time goes in v8:
time: 126 us; the launch traced here: 125 us
  blocking collectives  116 us (92%)
  Pallas kernels  8.97 us (7%)
    all_to_all x1, blocking collectives, on_device(): got = lax.all_to_all(sent, ('x', 'occ', 'rep', 'z'), 0, 0, tiled=True)  45.3 us
    all_to_all x1, blocking collectives, on_device(): lax.all_to_all(routed.reshape(VIR, SLOTS * GRP, LANE), ('z', 'x'), 0, 0,...  43.3 us
    all_to_all x1, blocking collectives, on_device(): parts = lax.all_to_all(copies, ('z', 'x'), 0, 0, tiled=True)  14.1 us
    all_to_all x1, blocking collectives, on_device(): parts = lax.all_to_all(pieces, ('rep', 'occ', 'x'), 0, 0, tiled=True)  12.9 us
    pallas_call x1, Pallas kernels, contract(): pl.pallas_call(contract_kernel, out_shape=jax.ShapeDtypeStruct((VIR, 8, L...  5.65 us

profile of v8, /device:TPU:0, one launch (start us, length us, event | category | flops | bytes accessed | tf_op | source)
XLA Modules:
  0.0 124.6 jit_solution(15523248499033807029)
XLA Ops:
  0.0 1.4 %spread.1 = f32[2048,128]{1,0:T(8,128)S(1)} custom-call(f32[64,4096]{1,0:T(8,128)} %bitcast.11), custom_call_target="tpu_custom_call" | custom-call | bytes 2097152 | tf_op jit(solution)/shard_map/spread/pallas_call | solution.py:40
  1.4 0.0 copy-start
  1.4 45.3 %all_to_all.20 = f32[256,8,128]{2,1,0:T(8,128)S(1)} all-to-all(f32[256,8,128]{2,1,0:T(8,128)S(1)} %bitcast.9), channel_id=1, replica_groups=mesh['x'=4,'z'=8,'occ'=4,'rep'=2] {'x','occ','rep','z'}, dimensions={0} | all-to-all | bytes 2097152 | tf_op jit(solution)/shard_map/all_to_all | solution.py:197
  46.7 0.0 copy-done
  46.7 1.3 %route.1 = f32[384,8,128]{2,1,0:T(8,128)S(1)} custom-call(s32[1,256]{1,0:T(1,128)S(1)} %bitcast.10, f32[2048,128]{1,0:T(8,128)S(1)} %bitcast.8), custom_call_target="tpu_custom_call" | custom-call | bytes 3145728 | tf_op jit(solution)/shard_map/route/pallas_call | solution.py:86
  48.0 43.3 %all_to_all.21 = f32[32,96,128]{2,1,0:T(8,128)S(1)} all-to-all(f32[32,96,128]{2,1,0:T(8,128)S(1)} %bitcast.6), channel_id=1, replica_groups=mesh['x'=4,'z'=8,'occ'=4,'rep'=2] {'z','x'}, dimensions={0} | all-to-all | bytes 3145728 | tf_op jit(solution)/shard_map/all_to_all | solution.py:199
  91.2 5.6 %contract.1 = f32[32,8,128]{2,1,0:T(8,128)S(1)} custom-call(f32[8,4,12,8,128]{4,3,2,1,0:T(8,128)S(1)} %bitcast.7, f32[12,512,512]{2,1,0:T(8,128)} %int_hbm.1), custom_call_target="tpu_custom_call" | custom-call | flops 1207959552 | bytes 14680064 | tf_op jit(solution)/shard_map/contract/pallas_call | solution.py:144
  96.9 12.9 %all_to_all.22.got_ref = f32[32,8,128]{2,1,0:T(8,128)S(1)} all-to-all(f32[32,8,128]{2,1,0:T(8,128)S(1)} %contract.1), channel_id=1, replica_groups=mesh['x'=4,'z'=8,'occ'=4,'rep'=2] {'rep','occ','x'}, dimensions={0} | all-to-all | bytes 262144 | tf_op jit(solution)/shard_map/all_to_all | solution.py:201
  109.8 14.1 %all_to_all.23.got_ref = f32[32,8,128]{2,1,0:T(8,128)S(1)} all-to-all(f32[32,8,128]{2,1,0:T(8,128)S(1)} %add_up_kernel.1), channel_id=1, replica_groups=mesh['x'=4,'z'=8,'occ'=4,'rep'=2] {'z','x'}, dimensions={0} | all-to-all | bytes 262144 | tf_op jit(solution)/shard_map/all_to_all | solution.py:203
  123.9 0.6 finish_kernel.1
  (1 shorter events, 0.0 us)
Async XLA Ops:
  1.4 45.3 %copy-start = (s32[256]{0:T(256)S(1)}, s32[256]{0:T(256)}, u32[]{:S(2)}) copy-start(s32[256]{0:T(256)} %param.5) | copy-start | bytes 3076
